TPU v7x, 512 devices: a whole 4x4x16 slice. The times are simulated.
512 devices in a mesh: gx: 8 (over z_lo), gy: 8 (over x, core), gz: 8 (over z_hi, y).
Axes of the slice: x: 4, y: 4, z: 16 (z_hi: 2, z_lo: 8; z = z_hi * 8 + z_lo), core: 2. Of those that a mesh axis runs over, the one named last changes fastest.
Arguments:
- tokens: bfloat16 [256, 8192], P(('gx', 'gy'), 'gz'), may hold values from -6 to 6
- gate_weight: bfloat16 [8192, 22528], P('gz', ('gx', 'gy')), may hold values from -0.0625 to 0.0625
- up_weight: bfloat16 [8192, 22528], P('gz', ('gx', 'gy')), may hold values from -0.0625 to 0.0625
- down_weight: bfloat16 [22528, 8192], P(('gx', 'gy'), 'gz'), may hold values from -0.0390625 to 0.0390625
- out_grad: bfloat16 [256, 8192], P(('gx', 'gy'), 'gz'), may hold values from -1.5 to 1.5
Outputs:
- mixed: bfloat16 [256, 8192], P(('gx', 'gy'), 'gz')
- tokens_grad: bfloat16 [256, 8192], P(('gx', 'gy'), 'gz')
- gate_grad: bfloat16 [8192, 22528], P('gz', ('gx', 'gy'))
- up_grad: bfloat16 [8192, 22528], P('gz', ('gx', 'gy'))
- down_grad: bfloat16 [22528, 8192], P(('gx', 'gy'), 'gz')
All inputs are finite; a program needn't handle non-finite values.
Results may differ from a plain program's by a relative error of at most 0.0049.
Values may be sent and summed in bfloat16 or wider, within the bound.
No kernel may reach another device: no remote copies, remote signals or barrier semaphores. Data moves between devices by JAX's collectives and lax.ppermute only.
A program may use at most 64 MiB of HBM per device.

v0:
```python
import jax
import jax.numpy as jnp
from jax import lax
from jax.sharding import PartitionSpec as P


def inner_share(first_part, second_part):
    return (
        lax.psum_scatter(first_part, "gz", scatter_dimension=0, tiled=True),
        lax.psum_scatter(second_part, "gz", scatter_dimension=0, tiled=True),
    )


def inner_rows(first_part, second_part):
    return (
        lax.all_gather(first_part, "gz", axis=0, tiled=True),
        lax.all_gather(second_part, "gz", axis=0, tiled=True),
    )


def feature_total(term_fn, row_count):
    return lax.psum_scatter(
        term_fn(jnp.int32(0), row_count * lax.axis_size(("gx", "gy"))),
        ("gx", "gy"),
        scatter_dimension=0,
        tiled=True,
    )


def gated(gate_val, up_val):
    sig_val = jax.nn.sigmoid(gate_val)
    return (gate_val * sig_val * up_val).astype(jnp.bfloat16)


def gated_back(hidden_grad, gate_val, up_val):
    sig_val = jax.nn.sigmoid(gate_val)
    up_diff = (hidden_grad * gate_val * sig_val).astype(jnp.bfloat16)
    gate_diff = (hidden_grad * up_val * sig_val * (1.0 + gate_val * (1.0 - sig_val))).astype(
        jnp.bfloat16
    )
    return (gate_diff, up_diff)


def contract_rows(left_mat, right_mat):
    return lax.dot_general(
        left_mat, right_mat, (((0,), (0,)), ((), ())), preferred_element_type=jnp.float32
    )


def contract_cols(left_mat, right_mat):
    return lax.dot_general(
        left_mat, right_mat, (((1,), (1,)), ((), ())), preferred_element_type=jnp.float32
    )


def on_device(tokens, gate_weight, up_weight, down_weight, out_grad):
    row_count = tokens.shape[0]
    tok_rows, grad_rows = (
        lax.all_gather(tokens, ("gx", "gy"), axis=0, tiled=True),
        lax.all_gather(out_grad, ("gx", "gy"), axis=0, tiled=True),
    )
    gate_part = jnp.dot(tok_rows, gate_weight, preferred_element_type=jnp.float32)
    up_part = jnp.dot(tok_rows, up_weight, preferred_element_type=jnp.float32)
    half_cols = gate_part.shape[1] // 2
    gate_share, up_share = inner_share(gate_part, up_part)
    hidden_share = gated(gate_share, up_share)
    lower_hidden, upper_hidden = inner_rows(
        hidden_share[:, :half_cols], hidden_share[:, half_cols:]
    )
    hidden = jnp.concatenate([lower_hidden, upper_hidden], axis=1)

    def forward_term(row_start, row_total):
        return jnp.dot(hidden, down_weight, preferred_element_type=jnp.float32)

    mixed = feature_total(forward_term, row_count).astype(jnp.bfloat16)
    down_grad = contract_rows(hidden, grad_rows).astype(jnp.bfloat16)
    hidden_part = contract_cols(grad_rows, down_weight)
    lower_grad, upper_grad = inner_share(hidden_part[:, :half_cols], hidden_part[:, half_cols:])
    hidden_grad = jnp.concatenate([lower_grad, upper_grad], axis=1)
    gate_share_diff, up_share_diff = gated_back(hidden_grad, gate_share, up_share)
    gate_diff, up_diff = inner_rows(gate_share_diff, up_share_diff)
    gate_grad = contract_rows(tok_rows, gate_diff).astype(jnp.bfloat16)
    up_grad = contract_rows(tok_rows, up_diff).astype(jnp.bfloat16)

    def backward_term(row_start, row_total):
        return contract_cols(gate_diff, gate_weight) + contract_cols(up_diff, up_weight)

    tokens_grad = feature_total(backward_term, row_count).astype(jnp.bfloat16)
    return (mixed, tokens_grad, gate_grad, up_grad, down_grad)


def solution(mesh):
    return jax.shard_map(
        on_device,
        mesh=mesh,
        in_specs=(
            P(("gx", "gy"), "gz"),
            P("gz", ("gx", "gy")),
            P("gz", ("gx", "gy")),
            P(("gx", "gy"), "gz"),
            P(("gx", "gy"), "gz"),
        ),
        out_specs=(
            P(("gx", "gy"), "gz"),
            P(("gx", "gy"), "gz"),
            P("gz", ("gx", "gy")),
            P("gz", ("gx", "gy")),
            P(("gx", "gy"), "gz"),
        ),
        check_vma=False,
    )
```

profile of v0, /device:TPU:24, one launch (start us, length us, event | category | flops | bytes accessed | tf_op | source)
XLA Modules:
  0.0 1264.0 jit_solution(1403177443391735919)
XLA Ops:
  7.2 0.0 reduce-scatter.11.cloned.1.call-start
  7.2 127.3 %all-gather.1 = bf16[64,4,1024]{2,1,0:T(4,128)(2,1)S(1)} all-gather(bf16[1,4,1024]{2,1,0:T(4,128)(2,1)} %bitcast.23), channel_id=1, replica_groups=mesh['gx'=8,'gy'=8,'gz'=8] {'gx','gy'}, dimensions={0}, use_global_device_ids=true | all-gather | bytes 532480 | tf_op jit(solution)/shard_map/all_gather | solution.py:60
  134.5 0.1 reshape.13
  134.7 0.5 fusion.9
  135.1 0.9 fusion.5
  136.0 0.0 reduce-scatter.9.cloned.1.call-start
  136.1 0.7 reduce-scatter.9.cloned.1.call-update
  136.8 0.0 reduce-scatter.5.cloned.1.call-start
  136.8 113.9 %all-gather = bf16[64,4,1024]{2,1,0:T(4,128)(2,1)S(1)} all-gather(bf16[1,4,1024]{2,1,0:T(4,128)(2,1)S(1)} %bitcast.24), channel_id=1, replica_groups=mesh['gx'=8,'gy'=8,'gz'=8] {'gx','gy'}, dimensions={0}, use_global_device_ids=true | all-gather | bytes 532480 | tf_op jit(solution)/shard_map/all_gather | solution.py:59
  250.8 0.1 reshape.11
  250.9 1.2 fusion.7
  252.1 0.0 reduce-scatter.7.cloned.1.call-start
  252.2 1.2 fusion.8
  253.4 1.3 dynamic-slice
  255.4 0.0 reduce-scatter.11.cloned.1.call-done
  255.4 88.5 %reduce-scatter.9.cloned.1.call-done = f32[32,176]{1,0:T(8,128)} async-done(((f32[256,176]{1,0:T(8,128)}), f32[32,176]{1,0:T(8,128)}) %reduce-scatter.9.cloned.1.call-update) | async-done | bytes 22544 | tf_op jit(solution)/shard_map/reduce_scatter | solution.py:9
  343.9 107.0 %reduce-scatter.5.cloned.1.call-done = f32[32,352]{1,0:T(8,128)} async-done(((f32[256,352]{1,0:T(8,128)}), f32[32,352]{1,0:T(8,128)}) %reduce-scatter.5.cloned.1.call-update) | async-done | bytes 45072 | tf_op jit(solution)/shard_map/reduce_scatter | solution.py:9
  450.9 106.6 %reduce-scatter.7.cloned.1.call-done = f32[32,352]{1,0:T(8,128)} async-done(((f32[256,352]{1,0:T(8,128)}), f32[32,352]{1,0:T(8,128)}) %reduce-scatter.7.cloned.1.call-update) | async-done | bytes 45072 | tf_op jit(solution)/shard_map/reduce_scatter | solution.py:10
  557.5 0.9 multiply_convert_fusion
  558.4 0.1 fusion.6
  558.5 63.0 %all_gather.19 = bf16[256,176]{1,0:T(8,128)(2,1)S(1)} all-gather(bf16[32,176]{1,0:T(8,128)(2,1)S(1)} %get-tuple-element.12), channel_id=1, replica_groups=mesh['gx'=8,'gy'=8,'gz'=8] {'gz'}, dimensions={0}, use_global_device_ids=true | all-gather | bytes 101376 | tf_op jit(solution)/shard_map/all_gather | solution.py:16
  621.5 63.0 %all_gather.20 = bf16[256,176]{1,0:T(8,128)(2,1)S(1)} all-gather(bf16[32,176]{1,0:T(8,128)(2,1)S(1)} %get-tuple-element.13), channel_id=1, replica_groups=mesh['gx'=8,'gy'=8,'gz'=8] {'gz'}, dimensions={0}, use_global_device_ids=true | all-gather | bytes 101376 | tf_op jit(solution)/shard_map/all_gather | solution.py:17
  684.5 0.5 fusion.2
  685.0 1.3 convolution_convert_fusion
  686.3 63.3 %all_gather.22 = bf16[256,352]{1,0:T(8,128)(2,1)S(1)} all-gather(bf16[32,352]{1,0:T(8,128)(2,1)S(1)} %get-tuple-element.10), channel_id=1, replica_groups=mesh['gx'=8,'gy'=8,'gz'=8] {'gz'}, dimensions={0}, use_global_device_ids=true | all-gather | bytes 202752 | tf_op jit(solution)/shard_map/all_gather | solution.py:16
  749.6 0.4 fusion.10
  750.1 1.2 fusion
  751.3 63.3 %all_gather.23 = bf16[256,352]{1,0:T(8,128)(2,1)S(1)} all-gather(bf16[32,352]{1,0:T(8,128)(2,1)S(1)} %get-tuple-element.9), channel_id=1, replica_groups=mesh['gx'=8,'gy'=8,'gz'=8] {'gz'}, dimensions={0}, use_global_device_ids=true | all-gather | bytes 202752 | tf_op jit(solution)/shard_map/all_gather | solution.py:17
  814.5 1.2 fusion.1
  815.8 0.4 convolution_add_fusion
  816.2 439.9 %all-reduce.4 = (bf16[256,1024]{1,0:T(8,128)(2,1)S(1)}, bf16[256,1024]{1,0:T(8,128)(2,1)}) all-reduce(f32[256,1024]{1,0:T(8,128)S(1)} %fusion.2, f32[256,1024]{1,0:T(8,128)S(1)} %convolution_add_fusion), channel_id=4, replica_groups=mesh['gx'=8,'gy'=8,'gz'=8] {'gx','gy'}, use_global_device_ids=true, to_apply=%region_2.0.clone | all-reduce | flops 524288 | bytes 3145728
  1256.2 1.3 dynamic-slice_convert_fusion
  (13 shorter events, 0.1 us)
Async XLA Ops:
  7.2 127.5 %copy-start = (bf16[352,1024]{1,0:T(8,128)(2,1)S(1)}, bf16[352,1024]{1,0:T(8,128)(2,1)}, u32[]{:S(2)}) copy-start(bf16[352,1024]{1,0:T(8,128)(2,1)} %param.8) | copy-start | bytes 2162692
  7.2 248.2 %reduce-scatter.11.cloned.1.call-start = ((), (), s32[]{:S(2)}) async-start(), calls=%async_computation.7 | async-start | bytes 294912 | tf_op jit(solution)/shard_map/reduce_scatter | solution.py:10
  135.1 1.7 copy-start.4
  136.0 114.9 %copy-start.1 = (bf16[1024,352]{0,1:T(8,128)(2,1)S(1)}, bf16[1024,352]{0,1:T(8,128)(2,1)}, u32[]{:S(2)}) copy-start(bf16[1024,352]{0,1:T(8,128)(2,1)} %param.6) | copy-start | bytes 2162692
  136.0 207.9 %reduce-scatter.9.cloned.1.call-start = ((), (), s32[]{:S(2)}) async-start(), calls=%async_computation.6 | async-start | bytes 294912 | tf_op jit(solution)/shard_map/reduce_scatter | solution.py:9
  136.8 314.1 %reduce-scatter.5.cloned.1.call-start = ((), (), s32[]{:S(2)}) async-start(), calls=%async_computation.4 | async-start | bytes 442368 | tf_op jit(solution)/shard_map/reduce_scatter | solution.py:9
  250.9 1.3 copy-start.2
  252.1 305.3 %reduce-scatter.7.cloned.1.call-start = ((), (), s32[]{:S(2)}) async-start(), calls=%async_computation.5 | async-start | bytes 442368 | tf_op jit(solution)/shard_map/reduce_scatter | solution.py:10
  751.3 64.5 %copy-start.3 = (bf16[1024,352]{0,1:T(8,128)(2,1)S(1)}, bf16[1024,352]{0,1:T(8,128)(2,1)}, u32[]{:S(2)}) copy-start(bf16[1024,352]{0,1:T(8,128)(2,1)} %param.7) | copy-start | bytes 2162692
Sparse Core Ops, SparseCore 0:
  136.1 102.4 reduce-scatter.10
  244.3 99.5 reduce-scatter.8
  348.9 101.8 reduce-scatter.4
  455.8 101.6 reduce-scatter.6
where the time goes:
time: 1260 us
  blocking collectives  934 us (74%)
  waiting for transfers between devices  303 us (24%)
  between operations  14.5 us (1%)
    unnamed x1, blocking collectives  440 us
    reduce_scatter x2, waiting for transfers between devices, inner_share(): lax.psum_scatter(first_part, 'gz', scatter_dimension=0, tiled=True)  195 us
    all_gather x1, blocking collectives, on_device(): lax.all_gather(out_grad, ('gx', 'gy'), axis=0, tiled=True)  127 us
    all_gather x2, blocking collectives, inner_rows(): lax.all_gather(first_part, 'gz', axis=0, tiled=True)  126 us
    all_gather x2, blocking collectives, inner_rows(): lax.all_gather(second_part, 'gz', axis=0, tiled=True)  126 us
    all_gather x1, blocking collectives, on_device(): lax.all_gather(tokens, ('gx', 'gy'), axis=0, tiled=True)  114 us
    reduce_scatter x2, waiting for transfers between devices, inner_share(): lax.psum_scatter(second_part, 'gz', scatter_dimension=0, tiled=True)  107 us
  transfers between devices with their start and end apart: 4, of which 3 were waited for; matrix products, arithmetic and copies ran while one was open for 0% of the time, Pallas kernels for 0%

commit v1 on v0

v1 whole, which is shorter than its diff:
```python
import jax
import jax.numpy as jnp
from jax import lax
from jax.sharding import Mesh, PartitionSpec as P

BF16 = jnp.bfloat16
F32 = jnp.float32


def dot(a, b, ca, cb):
    return lax.dot_general(a, b, (((ca,), (cb,)), ((), ())), preferred_element_type=F32)


def gather(part, axis):
    count = lax.axis_size(axis)
    return lax.all_to_all(jnp.broadcast_to(part[None], (count,) + part.shape), axis, 0, 0)


def swap(part, axis):
    return lax.ppermute(part, axis, [(0, 1), (1, 0)])


def on_device(tokens, gate_weight, up_weight, down_weight, out_grad):
    rows, width = tokens.shape
    n_gx, n_x, n_y = lax.axis_size("gx"), lax.axis_size("x"), lax.axis_size("y")
    units = gate_weight.shape[1]

    both = jnp.concatenate([tokens, out_grad], axis=0)
    both = gather(both, "gx").reshape(n_gx, 2, rows, width).transpose(1, 0, 2, 3)
    both = both.reshape(2, n_gx * rows, width)
    both = gather(both, "x").transpose(1, 0, 2, 3).reshape(2, n_x * n_gx * rows, width)
    other = swap(both, "core")
    tok_rows = jnp.concatenate([both[0], other[0]], axis=0)
    grad_rows = jnp.concatenate([both[1], other[1]], axis=0)
    total = tok_rows.shape[0]

    parts = jnp.stack(
        [
            dot(tok_rows, gate_weight, 1, 0).astype(BF16),
            dot(tok_rows, up_weight, 1, 0).astype(BF16),
            dot(grad_rows, down_weight, 1, 1).astype(BF16),
        ]
    )
    parts = parts.reshape(3, n_y, total // n_y, units).transpose(1, 0, 2, 3)
    share = lax.all_to_all(parts, "y", 0, 0).astype(F32).sum(axis=0)
    share = share + swap(share.astype(BF16), "zh").astype(F32)
    gate_val, up_val, hidden_grad = share[0], share[1], share[2]

    sig_val = jax.nn.sigmoid(gate_val)
    hidden = gate_val * sig_val * up_val
    up_diff = hidden_grad * gate_val * sig_val
    gate_diff = hidden_grad * up_val * sig_val * (1.0 + gate_val * (1.0 - sig_val))
    mid = jnp.stack([hidden, gate_diff, up_diff]).astype(BF16)
    mid = gather(mid, "y").transpose(1, 0, 2, 3).reshape(3, total, units)
    hidden, gate_diff, up_diff = mid[0], mid[1], mid[2]

    outs = jnp.stack(
        [
            dot(hidden, down_weight, 1, 0),
            dot(gate_diff, gate_weight, 1, 1) + dot(up_diff, up_weight, 1, 1),
        ]
    )
    half = total // 2
    outs = outs[:, :half] + swap(outs[:, half:], "core")
    outs = outs.astype(BF16).reshape(2, n_x, half // n_x, width).transpose(1, 0, 2, 3)
    outs = lax.all_to_all(outs, "x", 0, 0).astype(F32).sum(axis=0)
    outs = outs.reshape(2, n_gx, rows, width).transpose(1, 0, 2, 3)
    outs = lax.all_to_all(outs, "gx", 0, 0).sum(axis=0).astype(BF16)

    down_grad = dot(hidden, grad_rows, 0, 0).astype(BF16)
    gate_grad = dot(tok_rows, gate_diff, 0, 0).astype(BF16)
    up_grad = dot(tok_rows, up_diff, 0, 0).astype(BF16)
    return (outs[0], outs[1], gate_grad, up_grad, down_grad)


def solution(mesh):
    fine = Mesh(mesh.devices.reshape(8, 4, 2, 2, 4), ("gx", "x", "core", "zh", "y"))
    hid, dim = ("gx", "x", "core"), ("zh", "y")
    act = P(hid, dim)
    return jax.shard_map(
        on_device,
        mesh=fine,
        in_specs=(act, P(dim, hid), P(dim, hid), act, act),
        out_specs=(act, act, P(dim, hid), P(dim, hid), act),
        check_vma=False,
    )
```

time: 1260 us -> 138 us (0.11)
  blocking collectives: 934 us -> 73.5 us
  waiting for transfers between devices: 303 us -> 32.6 us
  starting transfers between devices: 0.16 us -> 15.9 us
  between operations: 14.5 us -> 0.92 us
    all_gather x6 -> x0, blocking collectives: 494 us -> none  [the longest x1 127 us: on_device(): lax.all_gather(out_grad, ('gx', 'gy'), axis=0, tiled=True)]
    unnamed x1 -> x0, blocking collectives: 440 us -> none
    reduce_scatter x4 -> x0, waiting for transfers between devices: 302 us -> none  [the longest x2 195 us: inner_share(): lax.psum_scatter(first_part, 'gz', scatter_dimension=0, tiled=True)]
    all_to_all x0 -> x5, blocking collectives: none -> 73.5 us  [the longest x3 48.1 us: gather(): lax.all_to_all(jnp.broadcast_to(part[None], (count,) + part.shape), axis,...]
    ppermute x0 -> x3, waiting for transfers between devices: none -> 20.1 us  [swap(): return lax.ppermute(part, axis, [(0, 1), (1, 0)])]
  transfers between devices with their start and end apart: 4 -> 4, of which waited for: 3 -> 4; matrix products, arithmetic and copies ran while one was open for 0% -> 3% of each run, Pallas kernels for 0% -> 0%
where the time goes in v1:
time: 138 us; the launch traced here: 136 us
  blocking collectives  73.5 us (53%)
  waiting for transfers between devices  32.6 us (24%)
  starting transfers between devices  15.9 us (12%)
  matrix products  6.87 us (5%)
  local copies, waits for them, and re-layouts  4.4 us (3%)
  other arithmetic  1.54 us (1%)
    all_to_all x3, blocking collectives, gather(): lax.all_to_all(jnp.broadcast_to(part[None], (count,) + part.shape), axis,...  48.1 us
    ppermute x3, waiting for transfers between devices, swap(): return lax.ppermute(part, axis, [(0, 1), (1, 0)])  20.1 us
    all_to_all x1, blocking collectives, on_device(): share = lax.all_to_all(parts, 'y', 0, 0).astype(F32).sum(axis=0)  12.9 us
    all_to_all x1, blocking collectives, on_device(): outs = lax.all_to_all(outs, 'x', 0, 0).astype(F32).sum(axis=0)  12.5 us
    all_to_all x1, waiting for transfers between devices, on_device(): outs = lax.all_to_all(outs, 'gx', 0, 0).sum(axis=0).astype(BF16)  12.4 us
    ppermute x3, starting transfers between devices, swap(): return lax.ppermute(part, axis, [(0, 1), (1, 0)])  12.1 us
    dot_general x9, matrix products, dot(): lax.dot_general(a, b, (((ca,), (cb,)), ((), ())), preferred_element_type=...  6.87 us
    all_to_all x1, starting transfers between devices, on_device(): outs = lax.all_to_all(outs, 'gx', 0, 0).sum(axis=0).astype(BF16)  3.84 us
  transfers between devices with their start and end apart: 4, of which 4 were waited for; matrix products, arithmetic and copies ran while one was open for 3% of the time, Pallas kernels for 0%

profile of v1, /device:TPU:24, one launch (start us, length us, event | category | flops | bytes accessed | tf_op | source)
XLA Modules:
  0.0 135.7 jit_solution(5031729276707232598)
XLA Ops:
  0.6 0.8 pad_maximum_fusion.6
  1.5 24.3 %all_to_all.30 = bf16[8,8,1024]{2,1,0:T(8,128)(2,1)S(1)} all-to-all(bf16[8,8,1024]{2,1,0:T(8,128)(2,1)S(1)} %broadcast_in_dim.8), channel_id=1, replica_groups=mesh['gx'=8,'x'=4,'core'=2,'zh'=2,'y'=4] {'gx'}, dimensions={0} | all-to-all | bytes 262144 | tf_op jit(solution)/shard_map/all_to_all | solution.py:16
  25.8 0.1 copy.39
  26.0 12.2 %all_to_all.31 = bf16[4,2,32,1024]{3,2,1,0:T(8,128)(2,1)S(1)} all-to-all(bf16[4,2,32,1024]{3,2,1,0:T(8,128)(2,1)S(1)} %broadcast_in_dim.10), channel_id=1, replica_groups=mesh['gx'=8,'x'=4,'core'=2,'zh'=2,'y'=4] {'x'}, dimensions={0} | all-to-all | bytes 1048576 | tf_op jit(solution)/shard_map/all_to_all | solution.py:16
  38.3 1.9 %collective-permute-start = (bf16[2,128,1024]{2,1,0:T(8,128)(2,1)S(1)}, bf16[2,128,1024]{2,1,0:T(8,128)(2,1)S(1)}, u32[]{:S(2)}, u32[]{:S(2)}) collective-permute-start(bf16[2,128,1024]{2,1,0:T(8,128)(2,1)S(1)} %bitcast.53), channel_id=1, source_target_pairs={{0,8},{8,0},{1,9},{9,1},{2,10},{10,2},{3,11},{11,3},{4,12},{12,4},... | collective-permute-start | bytes 1572872 | tf_op jit(solution)/shard_map/ppermute | solution.py:20
  40.2 1.8 %collective-permute-done = bf16[2,128,1024]{2,1,0:T(8,128)(2,1)S(1)} collective-permute-done((bf16[2,128,1024]{2,1,0:T(8,128)(2,1)S(1)}, bf16[2,128,1024]{2,1,0:T(8,128)(2,1)S(1)}, u32[]{:S(2)}, u32[]{:S(2)}) %collective-permute-start) | collective-permute-done | bytes 524320 | tf_op jit(solution)/shard_map/ppermute | solution.py:20
  42.2 0.4 convolution_convert_fusion.5
  42.6 0.2 copy.42
  42.8 0.6 copy-done.2
  43.4 1.1 convolution_convert_fusion.4
  44.5 1.1 copy.43
  45.6 0.4 convolution_convert_fusion.3
  46.0 0.2 copy.44
  46.4 12.9 %all_to_all.32 = bf16[4,3,64,352]{3,2,1,0:T(8,128)(2,1)S(1)} all-to-all(bf16[4,3,64,352]{3,2,1,0:T(8,128)(2,1)S(1)} %copy.45), channel_id=1, replica_groups=mesh['gx'=8,'x'=4,'core'=2,'zh'=2,'y'=4] {'y'}, dimensions={0} | all-to-all | bytes 1081344 | tf_op jit(solution)/shard_map/all_to_all | solution.py:45
  59.4 8.2 %collective-permute-start.1 = (bf16[3,64,352]{2,1,0:T(8,128)(2,1)S(1)}, bf16[3,64,352]{2,1,0:T(8,128)(2,1)S(1)}, u32[]{:S(2)}, u32[]{:S(2)}) collective-permute-start(bf16[3,64,352]{2,1,0:T(8,128)(2,1)S(1)} %convert_element_type.45), channel_id=1, source_target_pairs={{0,4},{4,0},{1,5},{5,1},{2,6},{6,2},{3,7},{7,3},{8,12},{12,8},{9,1... | collective-permute-start | bytes 405512 | tf_op jit(solution)/shard_map/ppermute | solution.py:20
  67.6 15.7 %collective-permute-done.1 = bf16[3,64,352]{2,1,0:T(8,128)(2,1)S(1)} collective-permute-done((bf16[3,64,352]{2,1,0:T(8,128)(2,1)S(1)}, bf16[3,64,352]{2,1,0:T(8,128)(2,1)S(1)}, u32[]{:S(2)}, u32[]{:S(2)}) %collective-permute-start.1) | collective-permute-done | bytes 135200 | tf_op jit(solution)/shard_map/ppermute | solution.py:20
  83.5 11.7 %all_to_all.33 = bf16[4,3,64,352]{3,2,1,0:T(8,128)(2,1)S(1)} all-to-all(bf16[4,3,64,352]{3,2,1,0:T(8,128)(2,1)S(1)} %broadcast_in_dim.22), channel_id=1, replica_groups=mesh['gx'=8,'x'=4,'core'=2,'zh'=2,'y'=4] {'y'}, dimensions={0} | all-to-all | bytes 1081344 | tf_op jit(solution)/shard_map/all_to_all | solution.py:16
  95.3 0.4 fusion.8
  95.7 0.4 convolution_bitcast_fusion
  96.1 0.4 fusion
  96.7 1.9 %collective-permute-start.2 = (f32[2,128,1024]{2,1,0:T(8,128)S(1)}, f32[2,128,1024]{2,1,0:T(8,128)S(1)}, u32[]{:S(2)}, u32[]{:S(2)}) collective-permute-start(f32[2,128,1024]{2,1,0:T(8,128)S(1)} %pad_maximum_fusion), channel_id=1, source_target_pairs={{0,8},{8,0},{1,9},{9,1},{2,10},{10,2},{3,11},{11,3},{4,12},{12,4},... | collective-permute-start | bytes 3145736 | tf_op jit(solution)/shard_map/ppermute | solution.py:20
  98.6 2.6 %collective-permute-done.2 = f32[2,128,1024]{2,1,0:T(8,128)S(1)} collective-permute-done((f32[2,128,1024]{2,1,0:T(8,128)S(1)}, f32[2,128,1024]{2,1,0:T(8,128)S(1)}, u32[]{:S(2)}, u32[]{:S(2)}) %collective-permute-start.2) | collective-permute-done | bytes 1048608 | tf_op jit(solution)/shard_map/ppermute | solution.py:20
  101.2 0.2 fusion.3
  101.4 12.5 %all_to_all.34 = bf16[4,2,32,1024]{3,2,1,0:T(8,128)(2,1)S(1)} all-to-all(bf16[4,2,32,1024]{3,2,1,0:T(8,128)(2,1)S(1)} %bitcast.55), channel_id=1, replica_groups=mesh['gx'=8,'x'=4,'core'=2,'zh'=2,'y'=4] {'x'}, dimensions={0} | all-to-all | bytes 1048576 | tf_op jit(solution)/shard_map/all_to_all | solution.py:66
  114.0 0.2 copy.47
  114.2 0.8 copy.48
  115.0 3.8 %all-to-all-start.5 = ((f32[8,2,4,1024]{3,2,1,0:T(4,128)}), f32[8,2,4,1024]{3,2,1,0:T(4,128)S(1)}, u32[]{:S(2)}, u32[]{:S(2)}) async-start(f32[8,2,4,1024]{3,2,1,0:T(4,128)} %copy.48), calls=%async_computation.5 | async-start | bytes 524288 | tf_op jit(solution)/shard_map/all_to_all | solution.py:68
  118.8 1.2 convolution_convert_fusion
  120.1 1.2 convolution_convert_fusion.1
  121.3 1.2 convolution_convert_fusion.2
  122.6 12.4 %all-to-all-done.5 = f32[8,2,4,1024]{3,2,1,0:T(4,128)S(1)} async-done(((f32[8,2,4,1024]{3,2,1,0:T(4,128)}), f32[8,2,4,1024]{3,2,1,0:T(4,128)S(1)}, u32[]{:S(2)}, u32[]{:S(2)}) %all-to-all-start.5) | async-done | bytes 262176 | tf_op jit(solution)/shard_map/all_to_all | solution.py:68
  135.0 0.6 slice_bitcast_fusion.2
  (33 shorter events, 1.2 us)
Async XLA Ops:
  0.6 41.5 %copy-start = (bf16[1024,352]{0,1:T(8,128)(2,1)S(1)}, bf16[1024,352]{0,1:T(8,128)(2,1)}, u32[]{:S(2)}) copy-start(bf16[1024,352]{0,1:T(8,128)(2,1)} %param.6) | copy-start | bytes 2162692
  38.3 3.8 %collective-permute-start = (bf16[2,128,1024]{2,1,0:T(8,128)(2,1)S(1)}, bf16[2,128,1024]{2,1,0:T(8,128)(2,1)S(1)}, u32[]{:S(2)}, u32[]{:S(2)}) collective-permute-start(bf16[2,128,1024]{2,1,0:T(8,128)(2,1)S(1)} %bitcast.53), channel_id=1, source_target_pairs={{0,8},{8,0},{1,9},{9,1},{2,10},{10,2},{3,11},{11,3},{4,12},{12,4},... | collective-permute-start | bytes 1572872 | tf_op jit(solution)/shard_map/ppermute | solution.py:20
  42.1 0.7 copy-start.3
  42.1 3.5 %copy-start.5 = (bf16[128,1024]{1,0:T(8,128)(2,1)}, bf16[128,1024]{1,0:T(8,128)(2,1)S(1)}, u32[]{:S(2)}) copy-start(bf16[128,1024]{1,0:T(8,128)(2,1)S(1)} %get-tuple-element.11) | copy-start | bytes 786436
  42.1 1.3 copy-start.2
  43.4 2.2 %copy-start.1 = (bf16[352,1024]{1,0:T(8,128)(2,1)S(1)}, bf16[352,1024]{1,0:T(8,128)(2,1)}, u32[]{:S(2)}) copy-start(bf16[352,1024]{1,0:T(8,128)(2,1)} %param.8) | copy-start | bytes 2162692
  59.4 23.9 %collective-permute-start.1 = (bf16[3,64,352]{2,1,0:T(8,128)(2,1)S(1)}, bf16[3,64,352]{2,1,0:T(8,128)(2,1)S(1)}, u32[]{:S(2)}, u32[]{:S(2)}) collective-permute-start(bf16[3,64,352]{2,1,0:T(8,128)(2,1)S(1)} %convert_element_type.45), channel_id=1, source_target_pairs={{0,4},{4,0},{1,5},{5,1},{2,6},{6,2},{3,7},{7,3},{8,12},{12,8},{9,1... | collective-permute-start | bytes 405512 | tf_op jit(solution)/shard_map/ppermute | solution.py:20
  96.7 4.6 %collective-permute-start.2 = (f32[2,128,1024]{2,1,0:T(8,128)S(1)}, f32[2,128,1024]{2,1,0:T(8,128)S(1)}, u32[]{:S(2)}, u32[]{:S(2)}) collective-permute-start(f32[2,128,1024]{2,1,0:T(8,128)S(1)} %pad_maximum_fusion), channel_id=1, source_target_pairs={{0,8},{8,0},{1,9},{9,1},{2,10},{10,2},{3,11},{11,3},{4,12},{12,4},... | collective-permute-start | bytes 3145736 | tf_op jit(solution)/shard_map/ppermute | solution.py:20
  113.9 4.9 %copy-start.6 = (bf16[128,1024]{1,0:T(8,128)(2,1)S(1)}, bf16[128,1024]{1,0:T(8,128)(2,1)}, u32[]{:S(2)}) copy-start(bf16[128,1024]{1,0:T(8,128)(2,1)} %copy-done.5) | copy-start | bytes 786436
  115.0 5.1 %copy-start.4 = (bf16[128,1024]{1,0:T(8,128)(2,1)S(1)}, bf16[128,1024]{1,0:T(8,128)(2,1)}, u32[]{:S(2)}) copy-start(bf16[128,1024]{1,0:T(8,128)(2,1)} %copy-done.3) | copy-start | bytes 786436
  115.0 20.0 %all-to-all-start.5 = ((f32[8,2,4,1024]{3,2,1,0:T(4,128)}), f32[8,2,4,1024]{3,2,1,0:T(4,128)S(1)}, u32[]{:S(2)}, u32[]{:S(2)}) async-start(f32[8,2,4,1024]{3,2,1,0:T(4,128)} %copy.48), calls=%async_computation.5 | async-start | bytes 524288 | tf_op jit(solution)/shard_map/all_to_all | solution.py:68

commit v2 on v1

v2 whole, which is shorter than its diff:
```python
import math

import jax
import jax.numpy as jnp
from jax import lax
from jax.sharding import Mesh, PartitionSpec as P

BF16 = jnp.bfloat16
F16 = jnp.float16
F32 = jnp.float32
LANES = 128


def dot(a, b, ca, cb):
    return lax.dot_general(a, b, (((ca,), (cb,)), ((), ())), preferred_element_type=F32)


def gather(part, axis):
    count = lax.axis_size(axis)
    return lax.all_to_all(jnp.broadcast_to(part[None], (count,) + part.shape), axis, 0, 0)


def swap(part, axis):
    return lax.ppermute(part, axis, [(0, 1), (1, 0)])


def scales(over):
    gate = 2.0 ** math.floor(math.log2(65504 / (over * 6 * 0.0625)))
    grad = 2.0 ** math.floor(math.log2(65504 / (over * 1.5 * 0.0390625)))
    return jnp.array([gate, gate, grad], F32)[:, None, None]


def on_device(tokens, gate_weight, up_weight, down_weight, out_grad):
    rows, width = tokens.shape
    n_gx, n_x, n_y = lax.axis_size("gx"), lax.axis_size("x"), lax.axis_size("y")
    units = gate_weight.shape[1]
    wide = -(-units // LANES) * LANES

    both = jnp.concatenate([tokens, out_grad], axis=0)
    both = gather(both, "gx").reshape(n_gx, 2, rows, width).transpose(1, 0, 2, 3)
    both = both.reshape(2, n_gx * rows, width)
    both = gather(both, "x").transpose(1, 0, 2, 3).reshape(2, n_x * n_gx * rows, width)
    other = swap(both, "core")
    tok_rows = jnp.concatenate([both[0], other[0]], axis=0)
    grad_rows = jnp.concatenate([both[1], other[1]], axis=0)
    total = tok_rows.shape[0]

    first, second = scales(width), scales(width * n_y)
    parts = jnp.stack([dot(tok_rows, gate_weight, 1, 0), dot(tok_rows, up_weight, 1, 0), dot(grad_rows, down_weight, 1, 1)])
    parts = jnp.pad((parts * first).astype(F16), ((0, 0), (0, 0), (0, wide - units)))
    parts = parts.reshape(3, n_y, total // n_y, wide).transpose(1, 0, 2, 3).reshape(n_y, -1, wide)
    share = lax.all_to_all(parts, "y", 0, 0).reshape(n_y, 3, -1, wide).astype(F32).sum(axis=0) / first
    away = swap((share * second).astype(F16).reshape(-1, wide), "zh").reshape(3, -1, wide)
    share = share + away.astype(F32) / second
    gate_val, up_val, hidden_grad = share[0], share[1], share[2]

    sig_val = jax.nn.sigmoid(gate_val)
    hidden = gate_val * sig_val * up_val
    up_diff = hidden_grad * gate_val * sig_val
    gate_diff = hidden_grad * up_val * sig_val * (1.0 + gate_val * (1.0 - sig_val))
    mid = jnp.stack([hidden, gate_diff, up_diff]).astype(BF16).reshape(-1, wide)
    mid = gather(mid, "y").reshape(n_y, 3, -1, wide).transpose(1, 0, 2, 3).reshape(3, total, wide)[:, :, :units]
    hidden, gate_diff, up_diff = mid[0], mid[1], mid[2]

    outs = jnp.stack(
        [
            dot(hidden, down_weight, 1, 0),
            dot(gate_diff, gate_weight, 1, 1) + dot(up_diff, up_weight, 1, 1),
        ]
    )
    half = total // 2
    outs = outs[:, :half] + swap(outs[:, half:].astype(BF16), "core").astype(F32)
    outs = outs.astype(BF16).reshape(2, n_x, half // n_x, width).transpose(1, 0, 2, 3)
    outs = lax.all_to_all(outs, "x", 0, 0).astype(F32).sum(axis=0)
    outs = outs.astype(BF16).reshape(2, n_gx, rows, width).transpose(1, 0, 2, 3)
    outs = outs.reshape(n_gx, 2 * rows, width)
    outs = lax.all_to_all(outs, "gx", 0, 0).astype(F32).sum(axis=0).astype(BF16)

    down_grad = dot(hidden, grad_rows, 0, 0).astype(BF16)
    gate_grad = dot(tok_rows, gate_diff, 0, 0).astype(BF16)
    up_grad = dot(tok_rows, up_diff, 0, 0).astype(BF16)
    return (outs[:rows], outs[rows:], gate_grad, up_grad, down_grad)


def solution(mesh):
    fine = Mesh(mesh.devices.reshape(8, 4, 2, 2, 4), ("gx", "x", "core", "zh", "y"))
    hid, dim = ("gx", "x", "core"), ("zh", "y")
    act = P(hid, dim)
    return jax.shard_map(
        on_device,
        mesh=fine,
        in_specs=(act, P(dim, hid), P(dim, hid), act, act),
        out_specs=(act, act, P(dim, hid), P(dim, hid), act),
        check_vma=False,
    )
```

time: 138 us -> 134 us (0.971)
  blocking collectives: 73.5 us -> 48.1 us
  waiting for transfers between devices: 32.6 us -> 45.3 us
  starting transfers between devices: 15.9 us -> 24.1 us
  local copies, waits for them, and re-layouts: 4.4 us -> 6.44 us
    all_to_all x2 -> x0, blocking collectives: 25.4 us -> none  [the longest x1 12.9 us: on_device(): share = lax.all_to_all(parts, 'y', 0, 0).astype(F32).sum(axis=0)]
    all_to_all x1 -> x3, waiting for transfers between devices: 12.4 us -> 25.9 us  [the longest x1 9.02 us: on_device(): outs = lax.all_to_all(outs, 'gx', 0, 0).astype(F32).sum(axis=0).astype(BF16)]
    all_to_all x1 -> x3, starting transfers between devices: 3.84 us -> 12 us  [the longest x1 4.82 us: on_device(): lax.all_to_all(parts, 'y', 0, 0).reshape(n_y, 3, -1, wide).astype(F32)]
    convert_element_type x3 -> x0, local copies, waits for them, and re-layouts: 1.41 us -> none  [the longest x1 1.08 us: on_device(): dot(tok_rows, up_weight, 1, 0).astype(BF16)]
  transfers between devices with their start and end apart: 4 -> 6, of which waited for: 4 -> 6; matrix products, arithmetic and copies ran while one was open for 3% -> 3% of each run, Pallas kernels for 0% -> 0%
where the time goes in v2:
time: 134 us; the launch traced here: 133 us
  blocking collectives  48.1 us (36%)
  waiting for transfers between devices  45.3 us (34%)
  starting transfers between devices  24.1 us (18%)
  local copies, waits for them, and re-layouts  6.44 us (5%)
  matrix products  6.2 us (5%)
  other arithmetic  1.67 us (1%)
    all_to_all x3, blocking collectives, gather(): lax.all_to_all(jnp.broadcast_to(part[None], (count,) + part.shape), axis,...  48.1 us
    ppermute x3, waiting for transfers between devices, swap(): return lax.ppermute(part, axis, [(0, 1), (1, 0)])  19.4 us
    ppermute x3, starting transfers between devices, swap(): return lax.ppermute(part, axis, [(0, 1), (1, 0)])  12.1 us
    all_to_all x1, waiting for transfers between devices, on_device(): outs = lax.all_to_all(outs, 'gx', 0, 0).astype(F32).sum(axis=0).astype(BF16)  9.02 us
    all_to_all x1, waiting for transfers between devices, on_device(): outs = lax.all_to_all(outs, 'x', 0, 0).astype(F32).sum(axis=0)  8.77 us
    all_to_all x1, waiting for transfers between devices, on_device(): lax.all_to_all(parts, 'y', 0, 0).reshape(n_y, 3, -1, wide).astype(F32)  8.1 us
    dot_general x9, matrix products, dot(): lax.dot_general(a, b, (((ca,), (cb,)), ((), ())), preferred_element_type=...  6.2 us
    all_to_all x1, starting transfers between devices, on_device(): lax.all_to_all(parts, 'y', 0, 0).reshape(n_y, 3, -1, wide).astype(F32)  4.82 us
  transfers between devices with their start and end apart: 6, of which 6 were waited for; matrix products, arithmetic and copies ran while one was open for 3% of the time, Pallas kernels for 0%

profile of v2, /device:TPU:24, one launch (start us, length us, event | category | flops | bytes accessed | tf_op | source)
XLA Modules:
  0.0 132.8 jit_solution(7171610398163864638)
XLA Ops:
  0.6 0.8 pad_maximum_fusion.6
  1.5 24.3 %all_to_all.30 = bf16[8,8,1024]{2,1,0:T(8,128)(2,1)S(1)} all-to-all(bf16[8,8,1024]{2,1,0:T(8,128)(2,1)S(1)} %broadcast_in_dim.8), channel_id=1, replica_groups=mesh['gx'=8,'x'=4,'core'=2,'zh'=2,'y'=4] {'gx'}, dimensions={0} | all-to-all | bytes 262144 | tf_op jit(solution)/shard_map/all_to_all | solution.py:20
  26.0 12.2 %all_to_all.31 = bf16[4,2,32,1024]{3,2,1,0:T(8,128)(2,1)S(1)} all-to-all(bf16[4,2,32,1024]{3,2,1,0:T(8,128)(2,1)S(1)} %broadcast_in_dim.10), channel_id=1, replica_groups=mesh['gx'=8,'x'=4,'core'=2,'zh'=2,'y'=4] {'x'}, dimensions={0} | all-to-all | bytes 1048576 | tf_op jit(solution)/shard_map/all_to_all | solution.py:20
  38.3 1.9 %collective-permute-start = (bf16[2,128,1024]{2,1,0:T(8,128)(2,1)S(1)}, bf16[2,128,1024]{2,1,0:T(8,128)(2,1)S(1)}, u32[]{:S(2)}, u32[]{:S(2)}) collective-permute-start(bf16[2,128,1024]{2,1,0:T(8,128)(2,1)S(1)} %bitcast.72), channel_id=1, source_target_pairs={{0,8},{8,0},{1,9},{9,1},{2,10},{10,2},{3,11},{11,3},{4,12},{12,4},... | collective-permute-start | bytes 1572872 | tf_op jit(solution)/shard_map/ppermute | solution.py:24
  40.2 1.8 %collective-permute-done = bf16[2,128,1024]{2,1,0:T(8,128)(2,1)S(1)} collective-permute-done((bf16[2,128,1024]{2,1,0:T(8,128)(2,1)S(1)}, bf16[2,128,1024]{2,1,0:T(8,128)(2,1)S(1)}, u32[]{:S(2)}, u32[]{:S(2)}) %collective-permute-start) | collective-permute-done | bytes 524320 | tf_op jit(solution)/shard_map/ppermute | solution.py:24
  42.1 0.4 convolution_bitcast_fusion.3
  42.5 0.9 copy-done.2
  43.4 0.4 convolution_bitcast_fusion.2
  43.9 0.7 copy-done.1
  44.5 0.4 convolution_bitcast_fusion.1
  45.1 0.5 copy.34
  45.8 0.9 copy.26
  46.7 4.8 %all-to-all-start.2 = ((f16[4,192,384]{2,1,0:T(8,128)(2,1)}), f16[4,192,384]{2,1,0:T(8,128)(2,1)S(1)}, u32[]{:S(2)}, u32[]{:S(2)}) async-start(f16[4,192,384]{2,1,0:T(8,128)(2,1)} %bitcast.14), calls=%async_computation.2 | async-start | bytes 1179648 | tf_op jit(solution)/shard_map/all_to_all | solution.py:52
  51.9 8.1 %all-to-all-done.2 = f16[4,192,384]{2,1,0:T(8,128)(2,1)S(1)} async-done(((f16[4,192,384]{2,1,0:T(8,128)(2,1)}), f16[4,192,384]{2,1,0:T(8,128)(2,1)S(1)}, u32[]{:S(2)}, u32[]{:S(2)}) %all-to-all-start.2) | async-done | bytes 589856 | tf_op jit(solution)/shard_map/all_to_all | solution.py:52
  60.2 8.2 %collective-permute-start.1 = (f16[192,384]{1,0:T(8,128)(2,1)S(1)}, f16[192,384]{1,0:T(8,128)(2,1)S(1)}, u32[]{:S(2)}, u32[]{:S(2)}) collective-permute-start(f16[192,384]{1,0:T(8,128)(2,1)S(1)} %multiply_convert_fusion), channel_id=1, source_target_pairs={{0,4},{4,0},{1,5},{5,1},{2,6},{6,2},{3,7},{7,3},{8,12},{12,8},{9,1... | collective-permute-start | bytes 442376 | tf_op jit(solution)/shard_map/ppermute | solution.py:24
  68.4 15.7 %collective-permute-done.1 = f16[192,384]{1,0:T(8,128)(2,1)S(1)} collective-permute-done((f16[192,384]{1,0:T(8,128)(2,1)S(1)}, f16[192,384]{1,0:T(8,128)(2,1)S(1)}, u32[]{:S(2)}, u32[]{:S(2)}) %collective-permute-start.1) | collective-permute-done | bytes 147488 | tf_op jit(solution)/shard_map/ppermute | solution.py:24
  84.4 11.7 %all_to_all.32 = bf16[4,192,384]{2,1,0:T(8,128)(2,1)S(1)} all-to-all(bf16[4,192,384]{2,1,0:T(8,128)(2,1)S(1)} %broadcast_in_dim.11), channel_id=1, replica_groups=mesh['gx'=8,'x'=4,'core'=2,'zh'=2,'y'=4] {'y'}, dimensions={0} | all-to-all | bytes 1179648 | tf_op jit(solution)/shard_map/all_to_all | solution.py:20
  96.1 0.4 fusion.7
  96.5 0.4 convolution_bitcast_fusion
  97.0 0.4 fusion
  97.5 1.9 %collective-permute-start.2 = (bf16[2,128,1024]{2,1,0:T(8,128)(2,1)S(1)}, bf16[2,128,1024]{2,1,0:T(8,128)(2,1)S(1)}, u32[]{:S(2)}, u32[]{:S(2)}) collective-permute-start(bf16[2,128,1024]{2,1,0:T(8,128)(2,1)S(1)} %fusion.5), channel_id=1, source_target_pairs={{0,8},{8,0},{1,9},{9,1},{2,10},{10,2},{3,11},{11,3},{4,12},{12,4},... | collective-permute-start | bytes 1572872 | tf_op jit(solution)/shard_map/ppermute | solution.py:24
  99.4 1.9 %collective-permute-done.2 = bf16[2,128,1024]{2,1,0:T(8,128)(2,1)S(1)} collective-permute-done((bf16[2,128,1024]{2,1,0:T(8,128)(2,1)S(1)}, bf16[2,128,1024]{2,1,0:T(8,128)(2,1)S(1)}, u32[]{:S(2)}, u32[]{:S(2)}) %collective-permute-start.2) | collective-permute-done | bytes 524320 | tf_op jit(solution)/shard_map/ppermute | solution.py:24
  101.5 0.8 copy.38
  102.3 3.5 %all-to-all-start.4 = ((bf16[4,2,32,1024]{3,2,1,0:T(8,128)(2,1)}), bf16[4,2,32,1024]{3,2,1,0:T(8,128)(2,1)S(1)}, u32[]{:S(2)}, u32[]{:S(2)}) async-start(bf16[4,2,32,1024]{3,2,1,0:T(8,128)(2,1)} %bitcast.61), calls=%async_computation.4 | async-start | bytes 1048576 | tf_op jit(solution)/shard_map/all_to_all | solution.py:74
  105.8 1.2 convolution_convert_fusion
  107.1 8.8 %all-to-all-done.4 = bf16[4,2,32,1024]{3,2,1,0:T(8,128)(2,1)S(1)} async-done(((bf16[4,2,32,1024]{3,2,1,0:T(8,128)(2,1)}), bf16[4,2,32,1024]{3,2,1,0:T(8,128)(2,1)S(1)}, u32[]{:S(2)}, u32[]{:S(2)}) %all-to-all-start.4) | async-done | bytes 524320 | tf_op jit(solution)/shard_map/all_to_all | solution.py:74
  116.1 0.7 copy.32
  116.9 3.7 %all-to-all-start.5 = ((bf16[8,8,1024]{2,1,0:T(8,128)(2,1)}), bf16[8,8,1024]{2,1,0:T(8,128)(2,1)S(1)}, u32[]{:S(2)}, u32[]{:S(2)}) async-start(bf16[8,8,1024]{2,1,0:T(8,128)(2,1)} %copy.32), calls=%async_computation.5 | async-start | bytes 262144 | tf_op jit(solution)/shard_map/all_to_all | solution.py:77
  120.6 1.3 convolution_convert_fusion.1
  121.9 1.2 convolution_convert_fusion.2
  123.1 9.0 %all-to-all-done.5 = bf16[8,8,1024]{2,1,0:T(8,128)(2,1)S(1)} async-done(((bf16[8,8,1024]{2,1,0:T(8,128)(2,1)}), bf16[8,8,1024]{2,1,0:T(8,128)(2,1)S(1)}, u32[]{:S(2)}, u32[]{:S(2)}) %all-to-all-start.5) | async-done | bytes 131104 | tf_op jit(solution)/shard_map/all_to_all | solution.py:77
  132.2 0.6 fusion.11
  (53 shorter events, 2.1 us)
Async XLA Ops:
  0.6 41.5 %copy-start = (bf16[1024,352]{0,1:T(8,128)(2,1)S(1)}, bf16[1024,352]{0,1:T(8,128)(2,1)}, u32[]{:S(2)}) copy-start(bf16[1024,352]{0,1:T(8,128)(2,1)} %param.8) | copy-start | bytes 2162692
  38.3 3.8 %collective-permute-start = (bf16[2,128,1024]{2,1,0:T(8,128)(2,1)S(1)}, bf16[2,128,1024]{2,1,0:T(8,128)(2,1)S(1)}, u32[]{:S(2)}, u32[]{:S(2)}) collective-permute-start(bf16[2,128,1024]{2,1,0:T(8,128)(2,1)S(1)} %bitcast.72), channel_id=1, source_target_pairs={{0,8},{8,0},{1,9},{9,1},{2,10},{10,2},{3,11},{11,3},{4,12},{12,4},... | collective-permute-start | bytes 1572872 | tf_op jit(solution)/shard_map/ppermute | solution.py:24
  40.2 3.6 %copy-start.5 = (bf16[1,4,32,1024]{3,2,1,0:T(8,128)(2,1)}, bf16[1,4,32,1024]{3,2,1,0:T(8,128)(2,1)S(1)}, u32[]{:S(2)}) copy-start(bf16[1,4,32,1024]{3,2,1,0:T(8,128)(2,1)S(1)} %get-tuple-element.6) | copy-start | bytes 786436
  42.1 1.7 %copy-start.3 = (bf16[128,1024]{1,0:T(8,128)(2,1)}, bf16[128,1024]{1,0:T(8,128)(2,1)S(1)}, u32[]{:S(2)}) copy-start(bf16[128,1024]{1,0:T(8,128)(2,1)S(1)} %get-tuple-element.7) | copy-start | bytes 786436
  42.1 1.7 %copy-start.7 = (bf16[128,1024]{1,0:T(8,128)(2,1)}, bf16[128,1024]{1,0:T(8,128)(2,1)S(1)}, u32[]{:S(2)}) copy-start(bf16[128,1024]{1,0:T(8,128)(2,1)S(1)} %get-tuple-element.8) | copy-start | bytes 786436
  42.1 1.3 copy-start.2
  43.4 1.1 copy-start.1
  43.8 1.1 copy-start.9
  45.8 5.8 %copy-start.10 = (f32[3]{0:T(128)S(1)}, f32[3]{0:T(128)}, u32[]{:S(2)}) copy-start(f32[3]{0:T(128)} %constant.14.clone) | copy-start | bytes 40
  45.8 5.9 %copy-start.11 = (f32[3]{0:T(128)S(1)}, f32[3]{0:T(128)}, u32[]{:S(2)}) copy-start(f32[3]{0:T(128)} %constant.15.clone) | copy-start | bytes 40
  46.7 37.4 %copy-start.12 = (f32[3]{0:T(128)S(1)}, f32[3]{0:T(128)}, u32[]{:S(2)}) copy-start(f32[3]{0:T(128)} %constant.23) | copy-start | bytes 40
  46.7 37.4 %copy-start.13 = (f32[3]{0:T(128)S(1)}, f32[3]{0:T(128)}, u32[]{:S(2)}) copy-start(f32[3]{0:T(128)} %constant.24) | copy-start | bytes 40
  46.7 13.2 %all-to-all-start.2 = ((f16[4,192,384]{2,1,0:T(8,128)(2,1)}), f16[4,192,384]{2,1,0:T(8,128)(2,1)S(1)}, u32[]{:S(2)}, u32[]{:S(2)}) async-start(f16[4,192,384]{2,1,0:T(8,128)(2,1)} %bitcast.14), calls=%async_computation.2 | async-start | bytes 1179648 | tf_op jit(solution)/shard_map/all_to_all | solution.py:52
  60.2 23.9 %collective-permute-start.1 = (f16[192,384]{1,0:T(8,128)(2,1)S(1)}, f16[192,384]{1,0:T(8,128)(2,1)S(1)}, u32[]{:S(2)}, u32[]{:S(2)}) collective-permute-start(f16[192,384]{1,0:T(8,128)(2,1)S(1)} %multiply_convert_fusion), channel_id=1, source_target_pairs={{0,4},{4,0},{1,5},{5,1},{2,6},{6,2},{3,7},{7,3},{8,12},{12,8},{9,1... | collective-permute-start | bytes 442376 | tf_op jit(solution)/shard_map/ppermute | solution.py:24
  97.5 3.8 %collective-permute-start.2 = (bf16[2,128,1024]{2,1,0:T(8,128)(2,1)S(1)}, bf16[2,128,1024]{2,1,0:T(8,128)(2,1)S(1)}, u32[]{:S(2)}, u32[]{:S(2)}) collective-permute-start(bf16[2,128,1024]{2,1,0:T(8,128)(2,1)S(1)} %fusion.5), channel_id=1, source_target_pairs={{0,8},{8,0},{1,9},{9,1},{2,10},{10,2},{3,11},{11,3},{4,12},{12,4},... | collective-permute-start | bytes 1572872 | tf_op jit(solution)/shard_map/ppermute | solution.py:24
  101.5 4.3 %copy-start.6 = (bf16[1,4,32,1024]{3,2,1,0:T(8,128)(2,1)S(1)}, bf16[1,4,32,1024]{3,2,1,0:T(8,128)(2,1)}, u32[]{:S(2)}) copy-start(bf16[1,4,32,1024]{3,2,1,0:T(8,128)(2,1)} %copy-done.5) | copy-start | bytes 786436
  101.5 4.3 %copy-start.8 = (bf16[128,1024]{1,0:T(8,128)(2,1)S(1)}, bf16[128,1024]{1,0:T(8,128)(2,1)}, u32[]{:S(2)}) copy-start(bf16[128,1024]{1,0:T(8,128)(2,1)} %copy-done.7) | copy-start | bytes 786436
  102.3 13.5 %all-to-all-start.4 = ((bf16[4,2,32,1024]{3,2,1,0:T(8,128)(2,1)}), bf16[4,2,32,1024]{3,2,1,0:T(8,128)(2,1)S(1)}, u32[]{:S(2)}, u32[]{:S(2)}) async-start(bf16[4,2,32,1024]{3,2,1,0:T(8,128)(2,1)} %bitcast.61), calls=%async_computation.4 | async-start | bytes 1048576 | tf_op jit(solution)/shard_map/all_to_all | solution.py:74
  107.1 13.6 %copy-start.4 = (bf16[128,1024]{1,0:T(8,128)(2,1)S(1)}, bf16[128,1024]{1,0:T(8,128)(2,1)}, u32[]{:S(2)}) copy-start(bf16[128,1024]{1,0:T(8,128)(2,1)} %copy-done.3) | copy-start | bytes 786436
  116.9 15.2 %all-to-all-start.5 = ((bf16[8,8,1024]{2,1,0:T(8,128)(2,1)}), bf16[8,8,1024]{2,1,0:T(8,128)(2,1)S(1)}, u32[]{:S(2)}, u32[]{:S(2)}) async-start(bf16[8,8,1024]{2,1,0:T(8,128)(2,1)} %copy.32), calls=%async_computation.5 | async-start | bytes 262144 | tf_op jit(solution)/shard_map/all_to_all | solution.py:77

commit v3 on v2

v3 whole, which is shorter than its diff:
```python
import functools
import math

import jax
import jax.numpy as jnp
from jax import lax
from jax.experimental import pallas as pl
from jax.experimental.pallas import tpu as pltpu
from jax.sharding import Mesh, PartitionSpec as P

BF16 = jnp.bfloat16
F16 = jnp.float16
F32 = jnp.float32
LANES = 128
VMEM = pl.BlockSpec(memory_space=pltpu.VMEM)
LIMIT = pltpu.CompilerParams(vmem_limit_bytes=40 * 1024 * 1024)


def dot(a, b, ca, cb):
    return lax.dot_general(a, b, (((ca,), (cb,)), ((), ())), preferred_element_type=F32)


def gather(part, axis):
    count = lax.axis_size(axis)
    return lax.all_to_all(jnp.broadcast_to(part[None], (count,) + part.shape), axis, 0, 0)


def swap(part, axis):
    return lax.ppermute(part, axis, [(0, 1), (1, 0)])


def scales(over):
    gate = 2.0 ** math.floor(math.log2(65504 / (over * 6 * 0.0625)))
    grad = 2.0 ** math.floor(math.log2(65504 / (over * 1.5 * 0.0390625)))
    return gate, gate, grad


def partial_sums(scale, chunks, rows_ref, gate_ref, up_ref, down_ref, out_ref):
    n_x, _, piece, width = rows_ref.shape
    units = gate_ref.shape[0]
    share = n_x * piece // chunks
    tok = rows_ref[:, 0].reshape(n_x * piece, width)
    grad = rows_ref[:, 1].reshape(n_x * piece, width)
    parts = (dot(tok, gate_ref[...], 1, 1), dot(tok, up_ref[...], 1, 1), dot(grad, down_ref[...], 1, 1))
    for which, part in enumerate(parts):
        part = (part * scale[which]).astype(out_ref.dtype)
        for chunk in range(chunks):
            rows = pl.ds(which * share, share)
            out_ref[chunk, rows, :units] = part[chunk * share : (chunk + 1) * share]
            out_ref[chunk, rows, units:] = jnp.zeros((share, out_ref.shape[2] - units), out_ref.dtype)


def partial_outs(n_x, mid_ref, gate_ref, up_ref, down_ref, out_ref):
    chunks, _, share, wide = mid_ref.shape
    units, width = down_ref.shape
    hidden, gate_diff, up_diff = [mid_ref[:, i].reshape(chunks * share, wide)[:, :units] for i in range(3)]
    mixed = dot(hidden, down_ref[...], 1, 0)
    back = dot(gate_diff, gate_ref[...], 1, 0) + dot(up_diff, up_ref[...], 1, 0)
    out_ref[:, 0] = mixed.astype(out_ref.dtype).reshape(n_x, -1, width)
    out_ref[:, 1] = back.astype(out_ref.dtype).reshape(n_x, -1, width)


def call(body, inputs, shape, dtype):
    return pl.pallas_call(
        body,
        out_shape=jax.ShapeDtypeStruct(shape, dtype),
        in_specs=[VMEM] * len(inputs),
        out_specs=VMEM,
        compiler_params=LIMIT,
    )(*inputs)


def on_device(tokens, gate_weight, up_weight, down_weight, out_grad):
    rows, width = tokens.shape
    n_gx, n_x, n_y = lax.axis_size("gx"), lax.axis_size("x"), lax.axis_size("y")
    units = gate_weight.shape[1]
    wide = -(-units // LANES) * LANES
    weights = (gate_weight.T, up_weight.T, down_weight)
    share = 2 * n_x * n_gx * rows // n_y
    near = n_y // 2

    both = jnp.concatenate([tokens, out_grad], axis=0)
    both = gather(both, "gx").reshape(n_gx, 2, rows, width).transpose(1, 0, 2, 3)
    own = gather(both.reshape(2, n_gx * rows, width), "x")
    other = swap(own, "core")

    first, second = scales(width), scales(width * n_y)
    sums = functools.partial(partial_sums, first, near)
    shape = (near, 3 * share, wide)
    parts = jnp.concatenate(
        [call(sums, (own,) + weights, shape, F32), call(sums, (other,) + weights, shape, F32)], axis=0
    )
    parts = lax.all_to_all(parts.astype(F16), "y", 0, 0).reshape(n_y, 3, share, wide).astype(F32).sum(axis=0)
    part = [parts[i] * (1.0 / first[i]) for i in range(3)]
    away = swap(jnp.concatenate([(part[i] * second[i]).astype(F16) for i in range(3)], axis=0), "zh")
    away = away.reshape(3, share, wide).astype(F32)
    gate_val, up_val, hidden_grad = [part[i] + away[i] * (1.0 / second[i]) for i in range(3)]

    sig_val = jax.nn.sigmoid(gate_val)
    hidden = gate_val * sig_val * up_val
    up_diff = hidden_grad * gate_val * sig_val
    gate_diff = hidden_grad * up_val * sig_val * (1.0 + gate_val * (1.0 - sig_val))
    mid = jnp.concatenate([hidden.astype(BF16), gate_diff.astype(BF16), up_diff.astype(BF16)], axis=0)
    mid = gather(mid, "y").reshape(n_y, 3, share, wide)

    body = functools.partial(partial_outs, n_x)
    away = swap(call(body, (mid[near:],) + weights, own.shape, BF16), "core")
    outs = call(body, (mid[:near],) + weights, own.shape, F32)
    outs = (outs + away.astype(F32)).astype(BF16)
    outs = lax.all_to_all(outs, "x", 0, 0).astype(F32).sum(axis=0)
    outs = outs.astype(BF16).reshape(2, n_gx, rows, width).transpose(1, 0, 2, 3)
    outs = outs.reshape(n_gx, 2 * rows, width)
    outs, mid, own, other = lax.optimization_barrier((outs, mid, own, other))
    outs = lax.all_to_all(outs, "gx", 0, 0).astype(F32).sum(axis=0).astype(BF16)

    total = n_y * share
    hidden, gate_diff, up_diff = [mid[:, i].reshape(total, wide)[:, :units] for i in range(3)]
    tok_rows, grad_rows = [
        jnp.concatenate([own[:, i].reshape(total // 2, width), other[:, i].reshape(total // 2, width)], axis=0)
        for i in range(2)
    ]
    down_grad = dot(hidden, grad_rows, 0, 0).astype(BF16)
    gate_grad = dot(gate_diff, tok_rows, 0, 0).astype(BF16)
    up_grad = dot(up_diff, tok_rows, 0, 0).astype(BF16)
    return (outs[:rows], outs[rows:], gate_grad.T, up_grad.T, down_grad)


def solution(mesh):
    fine = Mesh(mesh.devices.reshape(8, 4, 2, 2, 4), ("gx", "x", "core", "zh", "y"))
    hid, dim = ("gx", "x", "core"), ("zh", "y")
    act = P(hid, dim)
    return jax.shard_map(
        on_device,
        mesh=fine,
        in_specs=(act, P(dim, hid), P(dim, hid), act, act),
        out_specs=(act, act, P(dim, hid), P(dim, hid), act),
        check_vma=False,
    )
```

time: 134 us -> 128 us (0.955)
  blocking collectives: 48.1 us -> 73.6 us
  waiting for transfers between devices: 45.3 us -> 25.6 us
  starting transfers between devices: 24.1 us -> 15.8 us
  local copies, waits for them, and re-layouts: 6.44 us -> 2.14 us
  Pallas kernels: 0 us -> 2.79 us
  matrix products: 6.2 us -> 3.73 us
    all_to_all x0 -> x2, blocking collectives: none -> 25.4 us  [the longest x1 12.9 us: on_device(): lax.all_to_all(parts.astype(F16), 'y', 0, 0).reshape(n_y, 3, share, wide)]
    all_to_all x2 -> x0, waiting for transfers between devices: 16.9 us -> none  [the longest x1 8.77 us: on_device(): outs = lax.all_to_all(outs, 'x', 0, 0).astype(F32).sum(axis=0)]
    all_to_all x2 -> x0, starting transfers between devices: 8.29 us -> none  [the longest x1 4.82 us: on_device(): lax.all_to_all(parts, 'y', 0, 0).reshape(n_y, 3, -1, wide).astype(F32)]
    pallas_call x0 -> x4, Pallas kernels: none -> 2.79 us  [call(): pl.pallas_call(body, out_shape=jax.ShapeDtypeStruct(shape, dtype), in_spe...]
    dot_general x9 -> x3, matrix products: 6.2 us -> 3.73 us  [dot(): lax.dot_general(a, b, (((ca,), (cb,)), ((), ())), preferred_element_type=...]
    unnamed x29 -> x6, local copies, waits for them, and re-layouts: 2.12 us -> 0.02 us
    reshape x2 -> x0, local copies, waits for them, and re-layouts: 1.6 us -> none  [the longest x1 0.85 us: on_device(): outs.astype(BF16).reshape(2, n_x, half // n_x, width).transpose(1, 0, 2, 3)]
    ppermute x3, waiting for transfers between devices: 19.4 us -> 18 us  [swap(): return lax.ppermute(part, axis, [(0, 1), (1, 0)])]
  transfers between devices with their start and end apart: 6 -> 4, of which waited for: 6 -> 4; matrix products, arithmetic and copies ran while one was open for 3% -> 3% of each run, Pallas kernels for 0% -> 1%
where the time goes in v3:
time: 128 us; the launch traced here: 126 us
  blocking collectives  73.6 us (57%)
  waiting for transfers between devices  25.6 us (20%)
  starting transfers between devices  15.8 us (12%)
  matrix products  3.73 us (3%)
  Pallas kernels  2.79 us (2%)
  local copies, waits for them, and re-layouts  2.14 us (2%)
  other arithmetic  1.48 us (1%)
    all_to_all x3, blocking collectives, gather(): lax.all_to_all(jnp.broadcast_to(part[None], (count,) + part.shape), axis,...  48.2 us
    ppermute x3, waiting for transfers between devices, swap(): return lax.ppermute(part, axis, [(0, 1), (1, 0)])  18 us
    all_to_all x1, blocking collectives, on_device(): lax.all_to_all(parts.astype(F16), 'y', 0, 0).reshape(n_y, 3, share, wide)  12.9 us
    all_to_all x1, blocking collectives, on_device(): outs = lax.all_to_all(outs, 'x', 0, 0).astype(F32).sum(axis=0)  12.5 us
    ppermute x3, starting transfers between devices, swap(): return lax.ppermute(part, axis, [(0, 1), (1, 0)])  12.1 us
    all_to_all x1, waiting for transfers between devices, on_device(): outs = lax.all_to_all(outs, 'gx', 0, 0).astype(F32).sum(axis=0).astype(BF16)  7.62 us
    all_to_all x1, starting transfers between devices, on_device(): outs = lax.all_to_all(outs, 'gx', 0, 0).astype(F32).sum(axis=0).astype(BF16)  3.76 us
    dot_general x3, matrix products, dot(): lax.dot_general(a, b, (((ca,), (cb,)), ((), ())), preferred_element_type=...  3.73 us
  transfers between devices with their start and end apart: 4, of which 4 were waited for; matrix products, arithmetic and copies ran while one was open for 3% of the time, Pallas kernels for 1%

profile of v3, /device:TPU:24, one launch (start us, length us, event | category | flops | bytes accessed | tf_op | source)
XLA Modules:
  0.0 126.0 jit_solution(1447021358366108394)
XLA Ops:
  0.6 0.7 pad_maximum_fusion.6
  1.4 24.3 %all_to_all.30 = bf16[8,8,1024]{2,1,0:T(8,128)(2,1)S(1)} all-to-all(bf16[8,8,1024]{2,1,0:T(8,128)(2,1)S(1)} %broadcast_in_dim.8), channel_id=1, replica_groups=mesh['gx'=8,'x'=4,'core'=2,'zh'=2,'y'=4] {'gx'}, dimensions={0} | all-to-all | bytes 262144 | tf_op jit(solution)/shard_map/all_to_all | solution.py:25
  25.6 0.1 copy.13
  25.7 0.1 copy.14
  26.0 12.3 %all_to_all.31.rows_ref = bf16[4,2,32,1024]{3,2,1,0:T(8,128)(2,1)S(1)} all-to-all(bf16[4,2,32,1024]{3,2,1,0:T(8,128)(2,1)S(1)} %broadcast_in_dim.10), channel_id=1, replica_groups=mesh['gx'=8,'x'=4,'core'=2,'zh'=2,'y'=4] {'x'}, dimensions={0} | all-to-all | bytes 1048576 | tf_op jit(solution)/shard_map/all_to_all | solution.py:25
  38.3 1.9 %collective-permute-start = (bf16[4,2,32,1024]{3,2,1,0:T(8,128)(2,1)S(1)}, bf16[4,2,32,1024]{3,2,1,0:T(8,128)(2,1)S(1)}, u32[]{:S(2)}, u32[]{:S(2)}) collective-permute-start(bf16[4,2,32,1024]{3,2,1,0:T(8,128)(2,1)S(1)} %all_to_all.31.rows_ref), channel_id=1, source_target_pairs={{0,8},{8,0},{1,9},{9,1},{2,10},{10,2},{3,11},{11,3},{4,12},{12,4},... | collective-permute-start | bytes 1572872 | tf_op jit(solution)/shard_map/ppermute | solution.py:29
  40.3 0.8 shard_map.92
  41.1 1.0 collective-permute-done.rows_ref
  42.1 0.8 shard_map.93
  43.0 0.1 pad_maximum_fusion
  43.1 12.9 %all_to_all.32 = f16[4,192,384]{2,1,0:T(8,128)(2,1)S(1)} all-to-all(f16[4,192,384]{2,1,0:T(8,128)(2,1)S(1)} %pad_maximum_fusion), channel_id=1, replica_groups=mesh['gx'=8,'x'=4,'core'=2,'zh'=2,'y'=4] {'y'}, dimensions={0} | all-to-all | bytes 1179648 | tf_op jit(solution)/shard_map/all_to_all | solution.py:93
  56.2 8.2 %collective-permute-start.1 = (f16[192,384]{1,0:T(8,128)(2,1)S(1)}, f16[192,384]{1,0:T(8,128)(2,1)S(1)}, u32[]{:S(2)}, u32[]{:S(2)}) collective-permute-start(f16[192,384]{1,0:T(8,128)(2,1)S(1)} %pad_maximum_fusion.4), channel_id=1, source_target_pairs={{0,4},{4,0},{1,5},{5,1},{2,6},{6,2},{3,7},{7,3},{8,12},{12,8},{9,1... | collective-permute-start | bytes 442376 | tf_op jit(solution)/shard_map/ppermute | solution.py:29
  64.4 15.7 %collective-permute-done.1 = f16[192,384]{1,0:T(8,128)(2,1)S(1)} collective-permute-done((f16[192,384]{1,0:T(8,128)(2,1)S(1)}, f16[192,384]{1,0:T(8,128)(2,1)S(1)}, u32[]{:S(2)}, u32[]{:S(2)}) %collective-permute-start.1) | collective-permute-done | bytes 147488 | tf_op jit(solution)/shard_map/ppermute | solution.py:29
  80.1 0.1 multiply_convert_fusion.2
  80.3 11.6 %all_to_all.33 = bf16[4,192,384]{2,1,0:T(8,128)(2,1)S(1)} all-to-all(bf16[4,192,384]{2,1,0:T(8,128)(2,1)S(1)} %broadcast_in_dim.22), channel_id=1, replica_groups=mesh['gx'=8,'x'=4,'core'=2,'zh'=2,'y'=4] {'y'}, dimensions={0} | all-to-all | bytes 1179648 | tf_op jit(solution)/shard_map/all_to_all | solution.py:25
  92.0 0.6 shard_map.95
  92.6 1.9 %collective-permute-start.2 = (bf16[4,2,32,1024]{3,2,1,0:T(8,128)(2,1)S(1)}, bf16[4,2,32,1024]{3,2,1,0:T(8,128)(2,1)S(1)}, u32[]{:S(2)}, u32[]{:S(2)}) collective-permute-start(bf16[4,2,32,1024]{3,2,1,0:T(8,128)(2,1)S(1)} %shard_map.95), channel_id=1, source_target_pairs={{0,8},{8,0},{1,9},{9,1},{2,10},{10,2},{3,11},{11,3},{4,12},{12,4},... | collective-permute-start | bytes 1572872 | tf_op jit(solution)/shard_map/ppermute | solution.py:29
  94.5 0.6 shard_map.94
  95.1 1.3 %collective-permute-done.2 = bf16[4,2,32,1024]{3,2,1,0:T(8,128)(2,1)S(1)} collective-permute-done((bf16[4,2,32,1024]{3,2,1,0:T(8,128)(2,1)S(1)}, bf16[4,2,32,1024]{3,2,1,0:T(8,128)(2,1)S(1)}, u32[]{:S(2)}, u32[]{:S(2)}) %collective-permute-start.2) | collective-permute-done | bytes 524320 | tf_op jit(solution)/shard_map/ppermute | solution.py:29
  96.4 0.1 add_convert_fusion
  96.6 12.5 %all_to_all.34 = bf16[4,2,32,1024]{3,2,1,0:T(8,128)(2,1)S(1)} all-to-all(bf16[4,2,32,1024]{3,2,1,0:T(8,128)(2,1)S(1)} %add_convert_fusion), channel_id=1, replica_groups=mesh['gx'=8,'x'=4,'core'=2,'zh'=2,'y'=4] {'x'}, dimensions={0} | all-to-all | bytes 1048576 | tf_op jit(solution)/shard_map/all_to_all | solution.py:110
  109.0 0.1 reduce_sum.34
  109.1 0.1 copy.16
  109.2 0.1 copy.17
  109.3 0.7 copy.18
  110.0 3.8 %all-to-all-start.5 = ((bf16[8,8,1024]{2,1,0:T(8,128)(2,1)}), bf16[8,8,1024]{2,1,0:T(8,128)(2,1)S(1)}, u32[]{:S(2)}, u32[]{:S(2)}) async-start(bf16[8,8,1024]{2,1,0:T(8,128)(2,1)} %copy.18), calls=%async_computation.5 | async-start | bytes 262144 | tf_op jit(solution)/shard_map/all_to_all | solution.py:114
  113.9 0.1 fusion.14
  114.0 1.3 convolution_convert_fusion.1
  115.2 1.3 convolution_convert_fusion.2
  116.5 1.2 convolution_convert_fusion
  117.7 7.6 %all-to-all-done.5 = bf16[8,8,1024]{2,1,0:T(8,128)(2,1)S(1)} async-done(((bf16[8,8,1024]{2,1,0:T(8,128)(2,1)}), bf16[8,8,1024]{2,1,0:T(8,128)(2,1)S(1)}, u32[]{:S(2)}, u32[]{:S(2)}) %all-to-all-start.5) | async-done | bytes 131104 | tf_op jit(solution)/shard_map/all_to_all | solution.py:114
  125.4 0.6 fusion.16
  (20 shorter events, 0.6 us)
Async XLA Ops:
  25.7 14.5 %copy-start.2 = (bf16[352,1024]{1,0:T(8,128)(2,1)S(1)}, bf16[352,1024]{1,0:T(8,128)(2,1)}, u32[]{:S(2)}) copy-start(bf16[352,1024]{1,0:T(8,128)(2,1)} %down_ref.7) | copy-start | bytes 2162692
  25.9 14.4 %copy-start = (bf16[1024,352]{0,1:T(8,128)(2,1)S(1)}, bf16[1024,352]{0,1:T(8,128)(2,1)}, u32[]{:S(2)}) copy-start(bf16[1024,352]{0,1:T(8,128)(2,1)} %param.6) | copy-start | bytes 2162692
  25.9 14.4 %copy-start.1 = (bf16[1024,352]{0,1:T(8,128)(2,1)S(1)}, bf16[1024,352]{0,1:T(8,128)(2,1)}, u32[]{:S(2)}) copy-start(bf16[1024,352]{0,1:T(8,128)(2,1)} %param.7) | copy-start | bytes 2162692
  38.3 3.8 %collective-permute-start = (bf16[4,2,32,1024]{3,2,1,0:T(8,128)(2,1)S(1)}, bf16[4,2,32,1024]{3,2,1,0:T(8,128)(2,1)S(1)}, u32[]{:S(2)}, u32[]{:S(2)}) collective-permute-start(bf16[4,2,32,1024]{3,2,1,0:T(8,128)(2,1)S(1)} %all_to_all.31.rows_ref), channel_id=1, source_target_pairs={{0,8},{8,0},{1,9},{9,1},{2,10},{10,2},{3,11},{11,3},{4,12},{12,4},... | collective-permute-start | bytes 1572872 | tf_op jit(solution)/shard_map/ppermute | solution.py:29
  56.2 23.9 %collective-permute-start.1 = (f16[192,384]{1,0:T(8,128)(2,1)S(1)}, f16[192,384]{1,0:T(8,128)(2,1)S(1)}, u32[]{:S(2)}, u32[]{:S(2)}) collective-permute-start(f16[192,384]{1,0:T(8,128)(2,1)S(1)} %pad_maximum_fusion.4), channel_id=1, source_target_pairs={{0,4},{4,0},{1,5},{5,1},{2,6},{6,2},{3,7},{7,3},{8,12},{12,8},{9,1... | collective-permute-start | bytes 442376 | tf_op jit(solution)/shard_map/ppermute | solution.py:29
  92.6 3.8 %collective-permute-start.2 = (bf16[4,2,32,1024]{3,2,1,0:T(8,128)(2,1)S(1)}, bf16[4,2,32,1024]{3,2,1,0:T(8,128)(2,1)S(1)}, u32[]{:S(2)}, u32[]{:S(2)}) collective-permute-start(bf16[4,2,32,1024]{3,2,1,0:T(8,128)(2,1)S(1)} %shard_map.95), channel_id=1, source_target_pairs={{0,8},{8,0},{1,9},{9,1},{2,10},{10,2},{3,11},{11,3},{4,12},{12,4},... | collective-permute-start | bytes 1572872 | tf_op jit(solution)/shard_map/ppermute | solution.py:29
  110.0 15.3 %all-to-all-start.5 = ((bf16[8,8,1024]{2,1,0:T(8,128)(2,1)}), bf16[8,8,1024]{2,1,0:T(8,128)(2,1)S(1)}, u32[]{:S(2)}, u32[]{:S(2)}) async-start(bf16[8,8,1024]{2,1,0:T(8,128)(2,1)} %copy.18), calls=%async_computation.5 | async-start | bytes 262144 | tf_op jit(solution)/shard_map/all_to_all | solution.py:114

commit v4 on v3

v4 whole, which is shorter than its diff:
```python
import functools
import math

import jax
import jax.numpy as jnp
from jax import lax
from jax.experimental import pallas as pl
from jax.experimental.pallas import tpu as pltpu
from jax.sharding import Mesh, PartitionSpec as P

BF16 = jnp.bfloat16
F16 = jnp.float16
F32 = jnp.float32
LANES = 128
VMEM = pl.BlockSpec(memory_space=pltpu.VMEM)
LIMIT = pltpu.CompilerParams(vmem_limit_bytes=40 * 1024 * 1024)


def dot(a, b, ca, cb):
    return lax.dot_general(a, b, (((ca,), (cb,)), ((), ())), preferred_element_type=F32)


def gather(part, axis):
    count = lax.axis_size(axis)
    return lax.all_to_all(jnp.broadcast_to(part[None], (count,) + part.shape), axis, 0, 0)


def swap(part, axis):
    return lax.ppermute(part, axis, [(0, 1), (1, 0)])


def scales(over):
    gate = 2.0 ** math.floor(math.log2(65504 / (over * 6 * 0.0625)))
    grad = 2.0 ** math.floor(math.log2(65504 / (over * 1.5 * 0.0390625)))
    return gate, gate, grad


def pack(block):
    rows, units = block.shape
    full = units // LANES
    rest = units - full * LANES
    if not rest:
        return jnp.concatenate([block[:, i * LANES : (i + 1) * LANES] for i in range(full)], axis=0)
    gap = LANES - rest
    kept = rows * rest // LANES
    tail = block[:, full * LANES :]
    moved = jnp.concatenate([tail[kept:, i * gap : (i + 1) * gap] for i in range(rest // gap)], axis=0)
    last = jnp.concatenate([tail[:kept], moved], axis=1)
    return jnp.concatenate([block[:, i * LANES : (i + 1) * LANES] for i in range(full)] + [last], axis=0)


def unpack(block, rows, units):
    full = units // LANES
    rest = units - full * LANES
    parts = [block[i * rows : (i + 1) * rows] for i in range(full)]
    if rest:
        gap = LANES - rest
        kept = rows * rest // LANES
        last = block[full * rows :]
        moved = last[:, rest:]
        step = rows - kept
        back = jnp.concatenate([moved[i * step : (i + 1) * step] for i in range(rest // gap)], axis=1)
        parts.append(jnp.concatenate([last[:, :rest], back], axis=0))
    return jnp.concatenate(parts, axis=1)


def partial_sums(scale, chunks, rows_ref, gate_ref, up_ref, down_ref, out_ref):
    n_x, _, piece, width = rows_ref.shape
    share = n_x * piece // chunks
    tok = rows_ref[:, 0].reshape(n_x * piece, width)
    grad = rows_ref[:, 1].reshape(n_x * piece, width)
    parts = (dot(tok, gate_ref[...], 1, 1), dot(tok, up_ref[...], 1, 1), dot(grad, down_ref[...], 1, 1))
    for which, part in enumerate(parts):
        for chunk in range(chunks):
            out_ref[chunk, which] = pack(part[chunk * share : (chunk + 1) * share] * scale[which])


def partial_outs(n_x, mid_ref, gate_ref, up_ref, down_ref, out_ref, flat_ref):
    chunks = mid_ref.shape[0]
    _, total, units = flat_ref.shape
    width = down_ref.shape[1]
    share = total // chunks
    hidden, gate_diff, up_diff = [
        jnp.concatenate([unpack(mid_ref[chunk, which], share, units) for chunk in range(chunks)], axis=0)
        for which in range(3)
    ]
    mixed = dot(hidden, down_ref[...], 1, 0)
    back = dot(gate_diff, gate_ref[...], 1, 0) + dot(up_diff, up_ref[...], 1, 0)
    out_ref[:, 0] = mixed.astype(out_ref.dtype).reshape(n_x, -1, width)
    out_ref[:, 1] = back.astype(out_ref.dtype).reshape(n_x, -1, width)
    for which, rows in enumerate((hidden, gate_diff, up_diff)):
        flat_ref[which] = rows


def call(body, inputs, *outs):
    return pl.pallas_call(
        body,
        out_shape=[jax.ShapeDtypeStruct(shape, dtype) for shape, dtype in outs],
        in_specs=[VMEM] * len(inputs),
        out_specs=[VMEM] * len(outs),
        compiler_params=LIMIT,
    )(*inputs)


def on_device(tokens, gate_weight, up_weight, down_weight, out_grad):
    rows, width = tokens.shape
    n_gx, n_x, n_y = lax.axis_size("gx"), lax.axis_size("x"), lax.axis_size("y")
    units = gate_weight.shape[1]
    weights = (gate_weight.T, up_weight.T, down_weight)
    share = 2 * n_x * n_gx * rows // n_y
    near = n_y // 2

    both = jnp.concatenate([tokens, out_grad], axis=0)
    both = gather(both, "gx").reshape(n_gx, 2, rows, width).transpose(1, 0, 2, 3)
    own = gather(both.reshape(2, n_gx * rows, width), "x")
    other = swap(own, "core")

    first, second = scales(width), scales(width * n_y)
    sums = functools.partial(partial_sums, first, near)
    shape = (near, 3, share * units // LANES, LANES)
    parts = call(sums, (own,) + weights, (shape, F32)) + call(sums, (other,) + weights, (shape, F32))
    parts = jnp.concatenate(parts, axis=0).astype(F16)
    parts = lax.all_to_all(parts, "y", 0, 0).astype(F32).sum(axis=0)
    part = [parts[i] * (1.0 / first[i]) for i in range(3)]
    away = swap(jnp.stack([(part[i] * second[i]).astype(F16) for i in range(3)]), "zh").astype(F32)
    gate_val, up_val, hidden_grad = [part[i] + away[i] * (1.0 / second[i]) for i in range(3)]

    sig_val = jax.nn.sigmoid(gate_val)
    hidden = gate_val * sig_val * up_val
    up_diff = hidden_grad * gate_val * sig_val
    gate_diff = hidden_grad * up_val * sig_val * (1.0 + gate_val * (1.0 - sig_val))
    mid = gather(jnp.stack([hidden.astype(BF16), gate_diff.astype(BF16), up_diff.astype(BF16)]), "y")

    body = functools.partial(partial_outs, n_x)
    flat = ((3, near * share, units), BF16)
    away, far_mid = call(body, (mid[near:],) + weights, (own.shape, BF16), flat)
    away = swap(away, "core")
    outs, near_mid = call(body, (mid[:near],) + weights, (own.shape, F32), flat)
    outs = (outs + away.astype(F32)).astype(BF16)
    outs = lax.all_to_all(outs, "x", 0, 0).astype(F32).sum(axis=0)
    outs = outs.astype(BF16).reshape(2, n_gx, rows, width).transpose(1, 0, 2, 3)
    outs = outs.reshape(n_gx, 2 * rows, width)
    outs, near_mid, far_mid, own, other = lax.optimization_barrier((outs, near_mid, far_mid, own, other))
    outs = lax.all_to_all(outs, "gx", 0, 0).astype(F32).sum(axis=0).astype(BF16)

    half = near * share
    hidden, gate_diff, up_diff = [jnp.concatenate([near_mid[i], far_mid[i]], axis=0) for i in range(3)]
    tok_rows, grad_rows = [
        jnp.concatenate([own[:, i].reshape(half, width), other[:, i].reshape(half, width)], axis=0)
        for i in range(2)
    ]
    down_grad = dot(hidden, grad_rows, 0, 0).astype(BF16)
    gate_grad = dot(gate_diff, tok_rows, 0, 0).astype(BF16)
    up_grad = dot(up_diff, tok_rows, 0, 0).astype(BF16)
    return (outs[:rows], outs[rows:], gate_grad.T, up_grad.T, down_grad)


def solution(mesh):
    fine = Mesh(mesh.devices.reshape(8, 4, 2, 2, 4), ("gx", "x", "core", "zh", "y"))
    hid, dim = ("gx", "x", "core"), ("zh", "y")
    act = P(hid, dim)
    return jax.shard_map(
        on_device,
        mesh=fine,
        in_specs=(act, P(dim, hid), P(dim, hid), act, act),
        out_specs=(act, act, P(dim, hid), P(dim, hid), act),
        check_vma=False,
    )
```

time: 128 us -> 127 us (level)
  blocking collectives: 73.6 us -> 71.9 us
where the time goes in v4:
time: 127 us; the launch traced here: 125 us
  blocking collectives  71.9 us (57%)
  waiting for transfers between devices  24.7 us (19%)
  starting transfers between devices  17 us (13%)
  matrix products  3.73 us (3%)
  Pallas kernels  3.09 us (2%)
  local copies, waits for them, and re-layouts  2.14 us (2%)
  other arithmetic  1.48 us (1%)
    all_to_all x3, blocking collectives, gather(): lax.all_to_all(jnp.broadcast_to(part[None], (count,) + part.shape), axis,...  47.1 us
    ppermute x3, waiting for transfers between devices, swap(): return lax.ppermute(part, axis, [(0, 1), (1, 0)])  17 us
    all_to_all x1, blocking collectives, on_device(): outs = lax.all_to_all(outs, 'x', 0, 0).astype(F32).sum(axis=0)  12.5 us
    all_to_all x1, blocking collectives, on_device(): parts = lax.all_to_all(parts, 'y', 0, 0).astype(F32).sum(axis=0)  12.4 us
    ppermute x3, starting transfers between devices, swap(): return lax.ppermute(part, axis, [(0, 1), (1, 0)])  12 us
    all_to_all x1, waiting for transfers between devices, on_device(): outs = lax.all_to_all(outs, 'gx', 0, 0).astype(F32).sum(axis=0).astype(BF16)  7.62 us
    all_to_all x1, starting transfers between devices, on_device(): outs = lax.all_to_all(outs, 'gx', 0, 0).astype(F32).sum(axis=0).astype(BF16)  4.97 us
    dot_general x3, matrix products, dot(): lax.dot_general(a, b, (((ca,), (cb,)), ((), ())), preferred_element_type=...  3.73 us
  transfers between devices with their start and end apart: 4, of which 4 were waited for; matrix products, arithmetic and copies ran while one was open for 3% of the time, Pallas kernels for 1%

profile of v4, /device:TPU:24, one launch (start us, length us, event | category | flops | bytes accessed | tf_op | source)
XLA Modules:
  0.0 124.9 jit_solution(11683699916945157541)
XLA Ops:
  0.6 0.7 pad_maximum_fusion.6
  1.4 24.3 %all_to_all.30 = bf16[8,8,1024]{2,1,0:T(8,128)(2,1)S(1)} all-to-all(bf16[8,8,1024]{2,1,0:T(8,128)(2,1)S(1)} %broadcast_in_dim.8), channel_id=1, replica_groups=mesh['gx'=8,'x'=4,'core'=2,'zh'=2,'y'=4] {'gx'}, dimensions={0} | all-to-all | bytes 262144 | tf_op jit(solution)/shard_map/all_to_all | solution.py:25
  25.6 0.1 copy.13
  25.7 0.1 copy.14
  26.0 12.3 %all_to_all.31.rows_ref = bf16[4,2,32,1024]{3,2,1,0:T(8,128)(2,1)S(1)} all-to-all(bf16[4,2,32,1024]{3,2,1,0:T(8,128)(2,1)S(1)} %broadcast_in_dim.10), channel_id=1, replica_groups=mesh['gx'=8,'x'=4,'core'=2,'zh'=2,'y'=4] {'x'}, dimensions={0} | all-to-all | bytes 1048576 | tf_op jit(solution)/shard_map/all_to_all | solution.py:25
  38.3 1.9 %collective-permute-start = (bf16[4,2,32,1024]{3,2,1,0:T(8,128)(2,1)S(1)}, bf16[4,2,32,1024]{3,2,1,0:T(8,128)(2,1)S(1)}, u32[]{:S(2)}, u32[]{:S(2)}) collective-permute-start(bf16[4,2,32,1024]{3,2,1,0:T(8,128)(2,1)S(1)} %all_to_all.31.rows_ref), channel_id=1, source_target_pairs={{0,8},{8,0},{1,9},{9,1},{2,10},{10,2},{3,11},{11,3},{4,12},{12,4},... | collective-permute-start | bytes 1572872 | tf_op jit(solution)/shard_map/ppermute | solution.py:29
  40.3 1.0 shard_map.92
  41.3 0.8 collective-permute-done.rows_ref
  42.1 1.0 shard_map.93
  43.1 0.1 pad_maximum_fusion
  43.3 12.4 %all_to_all.32 = f16[4,3,176,128]{3,2,1,0:T(8,128)(2,1)S(1)} all-to-all(f16[4,3,176,128]{3,2,1,0:T(8,128)(2,1)S(1)} %pad_maximum_fusion), channel_id=1, replica_groups=mesh['gx'=8,'x'=4,'core'=2,'zh'=2,'y'=4] {'y'}, dimensions={0} | all-to-all | bytes 1081344 | tf_op jit(solution)/shard_map/all_to_all | solution.py:123
  55.8 8.2 %collective-permute-start.1 = (f16[3,176,128]{2,1,0:T(8,128)(2,1)S(1)}, f16[3,176,128]{2,1,0:T(8,128)(2,1)S(1)}, u32[]{:S(2)}, u32[]{:S(2)}) collective-permute-start(f16[3,176,128]{2,1,0:T(8,128)(2,1)S(1)} %pad_maximum_fusion.4), channel_id=1, source_target_pairs={{0,4},{4,0},{1,5},{5,1},{2,6},{6,2},{3,7},{7,3},{8,12},{12,8},{9,1... | collective-permute-start | bytes 405512 | tf_op jit(solution)/shard_map/ppermute | solution.py:29
  64.0 14.9 %collective-permute-done.1 = f16[3,176,128]{2,1,0:T(8,128)(2,1)S(1)} collective-permute-done((f16[3,176,128]{2,1,0:T(8,128)(2,1)S(1)}, f16[3,176,128]{2,1,0:T(8,128)(2,1)S(1)}, u32[]{:S(2)}, u32[]{:S(2)}) %collective-permute-start.1) | collective-permute-done | bytes 135200 | tf_op jit(solution)/shard_map/ppermute | solution.py:29
  79.0 0.1 multiply_convert_fusion.2
  79.2 10.5 %all_to_all.33 = bf16[4,3,176,128]{3,2,1,0:T(8,128)(2,1)S(1)} all-to-all(bf16[4,3,176,128]{3,2,1,0:T(8,128)(2,1)S(1)} %broadcast_in_dim.22), channel_id=1, replica_groups=mesh['gx'=8,'x'=4,'core'=2,'zh'=2,'y'=4] {'y'}, dimensions={0} | all-to-all | bytes 1081344 | tf_op jit(solution)/shard_map/all_to_all | solution.py:25
  89.8 0.6 shard_map.95
  90.3 1.9 %collective-permute-start.2 = (bf16[4,2,32,1024]{3,2,1,0:T(8,128)(2,1)S(1)}, bf16[4,2,32,1024]{3,2,1,0:T(8,128)(2,1)S(1)}, u32[]{:S(2)}, u32[]{:S(2)}) collective-permute-start(bf16[4,2,32,1024]{3,2,1,0:T(8,128)(2,1)S(1)} %get-tuple-element.15), channel_id=1, source_target_pairs={{0,8},{8,0},{1,9},{9,1},{2,10},{10,2},{3,11},{11,3},{4,12},{12,4},... | collective-permute-start | bytes 1572872 | tf_op jit(solution)/shard_map/ppermute | solution.py:29
  92.3 0.6 shard_map.94
  92.9 1.3 %collective-permute-done.2 = bf16[4,2,32,1024]{3,2,1,0:T(8,128)(2,1)S(1)} collective-permute-done((bf16[4,2,32,1024]{3,2,1,0:T(8,128)(2,1)S(1)}, bf16[4,2,32,1024]{3,2,1,0:T(8,128)(2,1)S(1)}, u32[]{:S(2)}, u32[]{:S(2)}) %collective-permute-start.2) | collective-permute-done | bytes 524320 | tf_op jit(solution)/shard_map/ppermute | solution.py:29
  94.2 0.1 add_convert_fusion
  94.3 12.5 %all_to_all.34 = bf16[4,2,32,1024]{3,2,1,0:T(8,128)(2,1)S(1)} all-to-all(bf16[4,2,32,1024]{3,2,1,0:T(8,128)(2,1)S(1)} %add_convert_fusion), channel_id=1, replica_groups=mesh['gx'=8,'x'=4,'core'=2,'zh'=2,'y'=4] {'x'}, dimensions={0} | all-to-all | bytes 1048576 | tf_op jit(solution)/shard_map/all_to_all | solution.py:140
  106.8 0.1 reduce_sum.34
  106.8 0.1 copy.16
  107.0 0.1 copy.17
  107.1 0.7 copy.18
  107.8 5.0 %all-to-all-start.5 = ((bf16[8,8,1024]{2,1,0:T(8,128)(2,1)}), bf16[8,8,1024]{2,1,0:T(8,128)(2,1)S(1)}, u32[]{:S(2)}, u32[]{:S(2)}) async-start(bf16[8,8,1024]{2,1,0:T(8,128)(2,1)} %copy.18), calls=%async_computation.5 | async-start | bytes 262144 | tf_op jit(solution)/shard_map/all_to_all | solution.py:144
  112.8 0.1 fusion.19
  112.9 1.3 %convolution_convert_fusion.1 = bf16[1024,352]{0,1:T(8,128)(2,1)} fusion(bf16[128,1024]{1,0:T(8,128)(2,1)S(1)} %bitcast.42, bf16[128,1024]{1,0:T(8,128)(2,1)S(1)} %bitcast.40, bf16[128,352]{1,0:T(8,128)(2,1)S(1)} %get-tuple-element.36, bf16[128,352]{1,0:T(8,128)(2,1)S(1)} %get-tuple-element.44), kind=kOutput, calls=%fused_computation.1 | convolution fusion | flops 186318848 | bytes 1425408 | tf_op jit(solution)/shard_map/dot_general | solution.py:20
  114.2 1.2 convolution_convert_fusion.2
  115.4 1.2 convolution_convert_fusion
  116.7 7.6 %all-to-all-done.5 = bf16[8,8,1024]{2,1,0:T(8,128)(2,1)S(1)} async-done(((bf16[8,8,1024]{2,1,0:T(8,128)(2,1)}), bf16[8,8,1024]{2,1,0:T(8,128)(2,1)S(1)}, u32[]{:S(2)}, u32[]{:S(2)}) %all-to-all-start.5) | async-done | bytes 131104 | tf_op jit(solution)/shard_map/all_to_all | solution.py:144
  124.3 0.6 fusion.21
  (20 shorter events, 0.6 us)
Async XLA Ops:
  25.7 14.5 %copy-start.2 = (bf16[352,1024]{1,0:T(8,128)(2,1)S(1)}, bf16[352,1024]{1,0:T(8,128)(2,1)}, u32[]{:S(2)}) copy-start(bf16[352,1024]{1,0:T(8,128)(2,1)} %down_ref.7) | copy-start | bytes 2162692
  25.9 14.4 %copy-start = (bf16[1024,352]{0,1:T(8,128)(2,1)S(1)}, bf16[1024,352]{0,1:T(8,128)(2,1)}, u32[]{:S(2)}) copy-start(bf16[1024,352]{0,1:T(8,128)(2,1)} %param.6) | copy-start | bytes 2162692
  25.9 14.4 %copy-start.1 = (bf16[1024,352]{0,1:T(8,128)(2,1)S(1)}, bf16[1024,352]{0,1:T(8,128)(2,1)}, u32[]{:S(2)}) copy-start(bf16[1024,352]{0,1:T(8,128)(2,1)} %param.7) | copy-start | bytes 2162692
  38.3 3.8 %collective-permute-start = (bf16[4,2,32,1024]{3,2,1,0:T(8,128)(2,1)S(1)}, bf16[4,2,32,1024]{3,2,1,0:T(8,128)(2,1)S(1)}, u32[]{:S(2)}, u32[]{:S(2)}) collective-permute-start(bf16[4,2,32,1024]{3,2,1,0:T(8,128)(2,1)S(1)} %all_to_all.31.rows_ref), channel_id=1, source_target_pairs={{0,8},{8,0},{1,9},{9,1},{2,10},{10,2},{3,11},{11,3},{4,12},{12,4},... | collective-permute-start | bytes 1572872 | tf_op jit(solution)/shard_map/ppermute | solution.py:29
  55.8 23.1 %collective-permute-start.1 = (f16[3,176,128]{2,1,0:T(8,128)(2,1)S(1)}, f16[3,176,128]{2,1,0:T(8,128)(2,1)S(1)}, u32[]{:S(2)}, u32[]{:S(2)}) collective-permute-start(f16[3,176,128]{2,1,0:T(8,128)(2,1)S(1)} %pad_maximum_fusion.4), channel_id=1, source_target_pairs={{0,4},{4,0},{1,5},{5,1},{2,6},{6,2},{3,7},{7,3},{8,12},{12,8},{9,1... | collective-permute-start | bytes 405512 | tf_op jit(solution)/shard_map/ppermute | solution.py:29
  90.3 3.8 %collective-permute-start.2 = (bf16[4,2,32,1024]{3,2,1,0:T(8,128)(2,1)S(1)}, bf16[4,2,32,1024]{3,2,1,0:T(8,128)(2,1)S(1)}, u32[]{:S(2)}, u32[]{:S(2)}) collective-permute-start(bf16[4,2,32,1024]{3,2,1,0:T(8,128)(2,1)S(1)} %get-tuple-element.15), channel_id=1, source_target_pairs={{0,8},{8,0},{1,9},{9,1},{2,10},{10,2},{3,11},{11,3},{4,12},{12,4},... | collective-permute-start | bytes 1572872 | tf_op jit(solution)/shard_map/ppermute | solution.py:29
  107.8 16.5 %all-to-all-start.5 = ((bf16[8,8,1024]{2,1,0:T(8,128)(2,1)}), bf16[8,8,1024]{2,1,0:T(8,128)(2,1)S(1)}, u32[]{:S(2)}, u32[]{:S(2)}) async-start(bf16[8,8,1024]{2,1,0:T(8,128)(2,1)} %copy.18), calls=%async_computation.5 | async-start | bytes 262144 | tf_op jit(solution)/shard_map/all_to_all | solution.py:144

commit v5 on v3

v5 whole, which is shorter than its diff:
```python
import functools
import math

import jax
import jax.numpy as jnp
from jax import lax
from jax.experimental import pallas as pl
from jax.experimental.pallas import tpu as pltpu
from jax.sharding import Mesh, PartitionSpec as P

BF16 = jnp.bfloat16
F16 = jnp.float16
F32 = jnp.float32
VMEM = pl.BlockSpec(memory_space=pltpu.VMEM)
LIMIT = pltpu.CompilerParams(vmem_limit_bytes=40 * 1024 * 1024)


def dot(a, b, ca, cb):
    return lax.dot_general(a, b, (((ca,), (cb,)), ((), ())), preferred_element_type=F32)


def gather(part, axis):
    count = lax.axis_size(axis)
    return lax.all_to_all(jnp.broadcast_to(part[None], (count,) + part.shape), axis, 0, 0)


def swap(part, axis):
    return lax.ppermute(part, axis, [(0, 1), (1, 0)])


def scales(over):
    gate = 2.0 ** math.floor(math.log2(65504 / (over * 6 * 0.0625)))
    grad = 2.0 ** math.floor(math.log2(65504 / (over * 1.5 * 0.0390625)))
    return gate, gate, grad


def partial_sums(scale, rows_ref, gate_ref, up_ref, down_ref, *rest):
    done_ref, out_ref = rest if len(rest) == 2 else (None, rest[0])
    n_x, _, piece, width = rows_ref.shape
    n_y, halves, _, share, _ = out_ref.shape
    tok = rows_ref[:, 0].reshape(n_x * piece, width)
    grad = rows_ref[:, 1].reshape(n_x * piece, width)
    for which, (weight_ref, rows) in enumerate(((gate_ref, tok), (up_ref, tok), (down_ref, grad))):
        part = dot(weight_ref[...], rows, 1, 1) * scale[which]
        for y in range(n_y):
            out_ref[y, halves - 1, which] = part[y * share : (y + 1) * share]
            if done_ref is not None:
                out_ref[y, 0, which] = done_ref[y, 0, which]


def all_units(mid_ref, half, which):
    blocks = [mid_ref[y, half, which].astype(F32) for y in range(mid_ref.shape[0])]
    return jnp.concatenate(blocks, axis=0).astype(BF16)


def partial_outs(half, mid_ref, gate_ref, up_ref, down_ref, out_ref):
    n_x, _, _, width = out_ref.shape
    hidden, gate_diff, up_diff = [all_units(mid_ref, half, which) for which in range(3)]
    mixed = dot(hidden, down_ref[...], 0, 0)
    back = dot(gate_diff, gate_ref[...], 0, 0) + dot(up_diff, up_ref[...], 0, 0)
    out_ref[:, 0] = mixed.astype(out_ref.dtype).reshape(n_x, -1, width)
    out_ref[:, 1] = back.astype(out_ref.dtype).reshape(n_x, -1, width)


def outs_and_grads(mid_ref, own_ref, other_ref, gate_ref, up_ref, down_ref, out_ref, *rest):
    hbm, (grad_ref, sems) = rest[:3], rest[3:]
    width = down_ref.shape[1]
    copies = []
    for which in range(3):
        kind = 1 if which == 0 else 0
        rows = [ref[:, kind].reshape(-1, width) for ref in (own_ref, other_ref)]
        diff = jnp.concatenate([all_units(mid_ref, half, which) for half in range(2)], axis=1)
        grad_ref[which] = dot(diff, jnp.concatenate(rows, axis=0), 1, 0).astype(BF16)
        copies.append(pltpu.make_async_copy(grad_ref.at[which], hbm[which], sems.at[which]))
        copies[-1].start()
    partial_outs(0, mid_ref, gate_ref, up_ref, down_ref, out_ref)
    for copy in copies:
        copy.wait()


def call(body, inputs, *outs):
    return pl.pallas_call(
        body,
        out_shape=[jax.ShapeDtypeStruct(shape, dtype) for shape, dtype in outs],
        in_specs=[VMEM] * len(inputs),
        out_specs=[VMEM] * len(outs),
        compiler_params=LIMIT,
    )(*inputs)


def on_device(tokens, gate_weight, up_weight, down_weight, out_grad):
    rows, width = tokens.shape
    n_gx, n_x, n_y = lax.axis_size("gx"), lax.axis_size("x"), lax.axis_size("y")
    units = gate_weight.shape[1]
    weights = (gate_weight.T, up_weight.T, down_weight)
    both = jnp.concatenate([tokens, out_grad], axis=0)
    both = gather(both, "gx").reshape(n_gx, 2, rows, width).transpose(1, 0, 2, 3)
    own = gather(both.reshape(2, n_gx * rows, width), "x")
    other = swap(own, "core")

    first = scales(width)
    share = units // n_y
    sums = functools.partial(partial_sums, first)
    half = n_x * n_gx * rows
    parts = call(sums, (own,) + weights, ((n_y, 1, 3, share, half), F32))
    parts = call(sums, (other,) + weights + tuple(parts), ((n_y, 2, 3, share, half), F32))[0]
    parts = lax.all_to_all(parts.astype(F16), "y", 0, 0).astype(F32).sum(axis=0) * (1.0 / n_y)
    parts = parts + swap(parts.astype(F16), "zh").astype(F32)
    gate_val, up_val, hidden_grad = [parts[:, i] * (n_y / first[i]) for i in range(3)]

    sig_val = jax.nn.sigmoid(gate_val)
    hidden = gate_val * sig_val * up_val
    up_diff = hidden_grad * gate_val * sig_val
    gate_diff = hidden_grad * up_val * sig_val * (1.0 + gate_val * (1.0 - sig_val))
    mid = jnp.stack([hidden.astype(BF16), gate_diff.astype(BF16), up_diff.astype(BF16)], axis=1)
    mid = gather(mid, "y")

    away = call(functools.partial(partial_outs, 1), (mid,) + weights, (own.shape, BF16))[0]
    away = swap(away, "core")
    inputs = (mid, own, other) + weights
    grads = jax.ShapeDtypeStruct(down_weight.shape, BF16)
    outs, down_grad, gate_grad, up_grad = pl.pallas_call(
        outs_and_grads,
        out_shape=[jax.ShapeDtypeStruct(own.shape, F32)] + [grads] * 3,
        in_specs=[VMEM] * len(inputs),
        out_specs=[VMEM] + [pl.BlockSpec(memory_space=pl.ANY)] * 3,
        scratch_shapes=[pltpu.VMEM((3,) + down_weight.shape, BF16), pltpu.SemaphoreType.DMA((3,))],
        compiler_params=LIMIT,
    )(*inputs)
    outs = (outs + away.astype(F32)).astype(BF16)
    outs = lax.all_to_all(outs, "x", 0, 0).astype(F32).sum(axis=0)
    outs = outs.astype(BF16).reshape(2, n_gx, rows, width).transpose(1, 0, 2, 3)
    outs = outs.reshape(n_gx, 2 * rows, width)
    outs = lax.all_to_all(outs, "gx", 0, 0).astype(F32).sum(axis=0).astype(BF16)

    return (outs[:rows], outs[rows:], gate_grad.T, up_grad.T, down_grad)


def solution(mesh):
    fine = Mesh(mesh.devices.reshape(8, 4, 2, 2, 4), ("gx", "x", "core", "zh", "y"))
    hid, dim = ("gx", "x", "core"), ("zh", "y")
    act = P(hid, dim)
    return jax.shard_map(
        on_device,
        mesh=fine,
        in_specs=(act, P(dim, hid), P(dim, hid), act, act),
        out_specs=(act, act, P(dim, hid), P(dim, hid), act),
        check_vma=False,
    )
```

time: 128 us -> 125 us (0.977)
  blocking collectives: 73.6 us -> 88.5 us
  waiting for transfers between devices: 25.6 us -> 16.2 us
  starting transfers between devices: 15.8 us -> 12 us
  matrix products: 3.73 us -> 0 us
    all_to_all x1 -> x2, blocking collectives: 12.9 us -> 28.7 us  [the longest x1 16.3 us: on_device(): outs = lax.all_to_all(outs, 'gx', 0, 0).astype(F32).sum(axis=0).astype(BF16)]
    all_to_all x1 -> x0, waiting for transfers between devices: 7.62 us -> none  [on_device(): outs = lax.all_to_all(outs, 'gx', 0, 0).astype(F32).sum(axis=0).astype(BF16)]
    all_to_all x1 -> x0, starting transfers between devices: 3.76 us -> none  [on_device(): outs = lax.all_to_all(outs, 'gx', 0, 0).astype(F32).sum(axis=0).astype(BF16)]
    dot_general x3 -> x0, matrix products: 3.73 us -> none  [dot(): lax.dot_general(a, b, (((ca,), (cb,)), ((), ())), preferred_element_type=...]
    ppermute x3, waiting for transfers between devices: 18 us -> 16.2 us  [swap(): return lax.ppermute(part, axis, [(0, 1), (1, 0)])]
  transfers between devices with their start and end apart: 4 -> 3, of which waited for: 4 -> 3; matrix products, arithmetic and copies ran while one was open for 3% -> 0% of each run, Pallas kernels for 1% -> 2%
where the time goes in v5:
time: 125 us; the launch traced here: 124 us
  blocking collectives  88.5 us (71%)
  waiting for transfers between devices  16.2 us (13%)
  starting transfers between devices  12 us (10%)
  Pallas kernels  3.76 us (3%)
  local copies, waits for them, and re-layouts  1.3 us (1%)
  other arithmetic  1.28 us (1%)
    all_to_all x3, blocking collectives, gather(): lax.all_to_all(jnp.broadcast_to(part[None], (count,) + part.shape), axis,...  47.1 us
    all_to_all x1, blocking collectives, on_device(): outs = lax.all_to_all(outs, 'gx', 0, 0).astype(F32).sum(axis=0).astype(BF16)  16.3 us
    ppermute x3, waiting for transfers between devices, swap(): return lax.ppermute(part, axis, [(0, 1), (1, 0)])  16.2 us
    all_to_all x1, blocking collectives, on_device(): outs = lax.all_to_all(outs, 'x', 0, 0).astype(F32).sum(axis=0)  12.7 us
    all_to_all x1, blocking collectives, on_device(): lax.all_to_all(parts.astype(F16), 'y', 0, 0).astype(F32).sum(axis=0)  12.4 us
    ppermute x3, starting transfers between devices, swap(): return lax.ppermute(part, axis, [(0, 1), (1, 0)])  12 us
  transfers between devices with their start and end apart: 3, of which 3 were waited for; matrix products, arithmetic and copies ran while one was open for 0% of the time, Pallas kernels for 2%

profile of v5, /device:TPU:24, one launch (start us, length us, event | category | flops | bytes accessed | tf_op | source)
XLA Modules:
  0.0 123.9 jit_solution(9798879088617608290)
XLA Ops:
  0.6 0.7 pad_maximum_fusion.1
  1.4 24.3 %all_to_all.30 = bf16[8,8,1024]{2,1,0:T(8,128)(2,1)S(1)} all-to-all(bf16[8,8,1024]{2,1,0:T(8,128)(2,1)S(1)} %broadcast_in_dim.8), channel_id=1, replica_groups=mesh['gx'=8,'x'=4,'core'=2,'zh'=2,'y'=4] {'gx'}, dimensions={0} | all-to-all | bytes 262144 | tf_op jit(solution)/shard_map/all_to_all | solution.py:24
  25.6 0.1 copy.13
  25.7 0.0 copy-start
  25.7 0.0 copy-start.1
  25.8 0.1 copy.14
  25.9 0.1 broadcast_in_dim.10
  26.0 12.3 %all_to_all.31.rows_ref.own_ref = bf16[4,2,32,1024]{3,2,1,0:T(8,128)(2,1)S(1)} all-to-all(bf16[4,2,32,1024]{3,2,1,0:T(8,128)(2,1)S(1)} %broadcast_in_dim.10), channel_id=1, replica_groups=mesh['gx'=8,'x'=4,'core'=2,'zh'=2,'y'=4] {'x'}, dimensions={0} | all-to-all | bytes 1048576 | tf_op jit(solution)/shard_map/all_to_all | solution.py:24
  38.3 1.9 %collective-permute-start = (bf16[4,2,32,1024]{3,2,1,0:T(8,128)(2,1)S(1)}, bf16[4,2,32,1024]{3,2,1,0:T(8,128)(2,1)S(1)}, u32[]{:S(2)}, u32[]{:S(2)}) collective-permute-start(bf16[4,2,32,1024]{3,2,1,0:T(8,128)(2,1)S(1)} %all_to_all.31.rows_ref.own_ref), channel_id=1, source_target_pairs={{0,8},{8,0},{1,9},{9,1},{2,10},{10,2},{3,11},{11,3},{4,12},{12,4},... | collective-permute-start | bytes 1572872 | tf_op jit(solution)/shard_map/ppermute | solution.py:28
  40.3 0.7 shard_map.92.rest_0_
  41.0 1.1 collective-permute-done.rows_ref.other_ref
  42.1 0.7 shard_map.93
  42.8 0.1 convert_element_type.34
  42.9 12.4 %all_to_all.32 = f16[4,2,3,88,128]{4,3,2,1,0:T(8,128)(2,1)S(1)} all-to-all(f16[4,2,3,88,128]{4,3,2,1,0:T(8,128)(2,1)S(1)} %convert_element_type.34), channel_id=1, replica_groups=mesh['gx'=8,'x'=4,'core'=2,'zh'=2,'y'=4] {'y'}, dimensions={0} | all-to-all | bytes 1081344 | tf_op jit(solution)/shard_map/all_to_all | solution.py:107
  55.3 0.1 convert_reduce_fusion
  55.4 8.2 %collective-permute-start.1 = (f16[2,3,88,128]{3,2,1,0:T(8,128)(2,1)S(1)}, f16[2,3,88,128]{3,2,1,0:T(8,128)(2,1)S(1)}, u32[]{:S(2)}, u32[]{:S(2)}) collective-permute-start(f16[2,3,88,128]{3,2,1,0:T(8,128)(2,1)S(1)} %multiply_convert_fusion), channel_id=1, source_target_pairs={{0,4},{4,0},{1,5},{5,1},{2,6},{6,2},{3,7},{7,3},{8,12},{12,8},{9,1... | collective-permute-start | bytes 405512 | tf_op jit(solution)/shard_map/ppermute | solution.py:28
  63.6 14.9 %collective-permute-done.1 = f16[2,3,88,128]{3,2,1,0:T(8,128)(2,1)S(1)} collective-permute-done((f16[2,3,88,128]{3,2,1,0:T(8,128)(2,1)S(1)}, f16[2,3,88,128]{3,2,1,0:T(8,128)(2,1)S(1)}, u32[]{:S(2)}, u32[]{:S(2)}) %collective-permute-start.1) | collective-permute-done | bytes 135200 | tf_op jit(solution)/shard_map/ppermute | solution.py:28
  78.6 0.1 multiply_convert_fusion.3
  78.7 0.1 broadcast_in_dim.22
  78.7 10.5 %all_to_all.33.mid_ref = bf16[4,2,3,88,128]{4,3,2,1,0:T(8,128)(2,1)S(1)} all-to-all(bf16[4,2,3,88,128]{4,3,2,1,0:T(8,128)(2,1)S(1)} %broadcast_in_dim.22), channel_id=1, replica_groups=mesh['gx'=8,'x'=4,'core'=2,'zh'=2,'y'=4] {'y'}, dimensions={0} | all-to-all | bytes 1081344 | tf_op jit(solution)/shard_map/all_to_all | solution.py:24
  89.3 0.6 shard_map.95
  89.9 1.9 %collective-permute-start.2 = (bf16[4,2,32,1024]{3,2,1,0:T(8,128)(2,1)S(1)}, bf16[4,2,32,1024]{3,2,1,0:T(8,128)(2,1)S(1)}, u32[]{:S(2)}, u32[]{:S(2)}) collective-permute-start(bf16[4,2,32,1024]{3,2,1,0:T(8,128)(2,1)S(1)} %shard_map.95), channel_id=1, source_target_pairs={{0,8},{8,0},{1,9},{9,1},{2,10},{10,2},{3,11},{11,3},{4,12},{12,4},... | collective-permute-start | bytes 1572872 | tf_op jit(solution)/shard_map/ppermute | solution.py:28
  91.8 1.7 %shard_map.94 = (f32[4,2,32,1024]{3,2,1,0:T(8,128)S(1)}, bf16[352,1024]{1,0:T(8,128)(2,1)}, bf16[352,1024]{1,0:T(8,128)(2,1)}, bf16[352,1024]{1,0:T(8,128)(2,1)}) custom-call(bf16[4,2,3,88,128]{4,3,2,1,0:T(8,128)(2,1)S(1)} %all_to_all.33.mid_ref, bf16[4,2,32,1024]{3,2,1,0:T(8,128)(2,1)S(1)} %all_to_all.31.rows_ref.own_ref, ...), custom_call_target="tpu_custom_call" | custom-call | tf_op jit(solution)/shard_map/pallas_call | solution.py:122
  93.5 0.2 collective-permute-done.2
  93.7 0.1 add_convert_fusion
  93.8 12.7 %all_to_all.34 = bf16[4,2,32,1024]{3,2,1,0:T(8,128)(2,1)S(1)} all-to-all(bf16[4,2,32,1024]{3,2,1,0:T(8,128)(2,1)S(1)} %add_convert_fusion), channel_id=1, replica_groups=mesh['gx'=8,'x'=4,'core'=2,'zh'=2,'y'=4] {'x'}, dimensions={0} | all-to-all | bytes 1048576 | tf_op jit(solution)/shard_map/all_to_all | solution.py:131
  106.5 0.1 reduce_sum.34
  106.6 0.1 copy.16
  106.7 0.1 copy.17
  106.8 0.1 copy.18
  106.9 16.3 %all_to_all.35 = bf16[8,8,1024]{2,1,0:T(8,128)(2,1)S(1)} all-to-all(bf16[8,8,1024]{2,1,0:T(8,128)(2,1)S(1)} %copy.18), channel_id=1, replica_groups=mesh['gx'=8,'x'=4,'core'=2,'zh'=2,'y'=4] {'gx'}, dimensions={0} | all-to-all | bytes 262144 | tf_op jit(solution)/shard_map/all_to_all | solution.py:134
  123.3 0.6 fusion
  (10 shorter events, 0.2 us)
Async XLA Ops:
  25.7 14.5 %copy-start = (bf16[1024,352]{0,1:T(8,128)(2,1)S(1)}, bf16[1024,352]{0,1:T(8,128)(2,1)}, u32[]{:S(2)}) copy-start(bf16[1024,352]{0,1:T(8,128)(2,1)} %param.6) | copy-start | bytes 2162692
  25.7 14.5 %copy-start.1 = (bf16[1024,352]{0,1:T(8,128)(2,1)S(1)}, bf16[1024,352]{0,1:T(8,128)(2,1)}, u32[]{:S(2)}) copy-start(bf16[1024,352]{0,1:T(8,128)(2,1)} %param.7) | copy-start | bytes 2162692
  25.8 14.5 %copy-start.2 = (bf16[352,1024]{1,0:T(8,128)(2,1)S(1)}, bf16[352,1024]{1,0:T(8,128)(2,1)}, u32[]{:S(2)}) copy-start(bf16[352,1024]{1,0:T(8,128)(2,1)} %down_ref.7) | copy-start | bytes 2162692
  38.3 3.8 %collective-permute-start = (bf16[4,2,32,1024]{3,2,1,0:T(8,128)(2,1)S(1)}, bf16[4,2,32,1024]{3,2,1,0:T(8,128)(2,1)S(1)}, u32[]{:S(2)}, u32[]{:S(2)}) collective-permute-start(bf16[4,2,32,1024]{3,2,1,0:T(8,128)(2,1)S(1)} %all_to_all.31.rows_ref.own_ref), channel_id=1, source_target_pairs={{0,8},{8,0},{1,9},{9,1},{2,10},{10,2},{3,11},{11,3},{4,12},{12,4},... | collective-permute-start | bytes 1572872 | tf_op jit(solution)/shard_map/ppermute | solution.py:28
  55.4 23.1 %collective-permute-start.1 = (f16[2,3,88,128]{3,2,1,0:T(8,128)(2,1)S(1)}, f16[2,3,88,128]{3,2,1,0:T(8,128)(2,1)S(1)}, u32[]{:S(2)}, u32[]{:S(2)}) collective-permute-start(f16[2,3,88,128]{3,2,1,0:T(8,128)(2,1)S(1)} %multiply_convert_fusion), channel_id=1, source_target_pairs={{0,4},{4,0},{1,5},{5,1},{2,6},{6,2},{3,7},{7,3},{8,12},{12,8},{9,1... | collective-permute-start | bytes 405512 | tf_op jit(solution)/shard_map/ppermute | solution.py:28
  89.9 3.8 %collective-permute-start.2 = (bf16[4,2,32,1024]{3,2,1,0:T(8,128)(2,1)S(1)}, bf16[4,2,32,1024]{3,2,1,0:T(8,128)(2,1)S(1)}, u32[]{:S(2)}, u32[]{:S(2)}) collective-permute-start(bf16[4,2,32,1024]{3,2,1,0:T(8,128)(2,1)S(1)} %shard_map.95), channel_id=1, source_target_pairs={{0,8},{8,0},{1,9},{9,1},{2,10},{10,2},{3,11},{11,3},{4,12},{12,4},... | collective-permute-start | bytes 1572872 | tf_op jit(solution)/shard_map/ppermute | solution.py:28

commit v6 on v5

v6 whole, which is shorter than its diff:
```python
import functools
import math

import jax
import jax.numpy as jnp
from jax import lax
from jax.experimental import pallas as pl
from jax.experimental.pallas import tpu as pltpu
from jax.sharding import Mesh, PartitionSpec as P

BF16 = jnp.bfloat16
F16 = jnp.float16
F32 = jnp.float32
VMEM = pl.BlockSpec(memory_space=pltpu.VMEM)
LIMIT = pltpu.CompilerParams(vmem_limit_bytes=20 * 1024 * 1024)


def dot(a, b, ca, cb):
    return lax.dot_general(a, b, (((ca,), (cb,)), ((), ())), preferred_element_type=F32)


def gather(part, axis):
    count = lax.axis_size(axis)
    return lax.all_to_all(jnp.broadcast_to(part[None], (count,) + part.shape), axis, 0, 0)


def swap(part, axis):
    return lax.ppermute(part, axis, [(0, 1), (1, 0)])


def scales(over):
    gate = 2.0 ** math.floor(math.log2(65504 / (over * 6 * 0.0625)))
    grad = 2.0 ** math.floor(math.log2(65504 / (over * 1.5 * 0.0390625)))
    return gate, gate, grad


def partial_sums(scale, rows_ref, mine_ref, peer_ref, out_ref):
    n_x, _, piece, width = rows_ref.shape
    n_y, _, _, share, _ = out_ref.shape
    tok = rows_ref[:, 0].reshape(n_x * piece, width)
    grad = rows_ref[:, 1].reshape(n_x * piece, width)
    for core, ref in enumerate((mine_ref, peer_ref)):
        for which, rows in enumerate((tok, tok, grad)):
            part = dot(ref[which], rows, 1, 1) * scale[which]
            for y in range(n_y):
                out_ref[y, core, which] = part[y * share : (y + 1) * share]


def all_units(mid_ref, *where):
    blocks = [mid_ref[(y,) + where].astype(F32) for y in range(mid_ref.shape[0])]
    return jnp.concatenate(blocks, axis=0).astype(BF16)


def partial_outs(mid_ref, own_ref, mine_ref, peer_ref, out_ref, give_ref):
    n_x, _, piece, width = out_ref.shape
    n_y, _, _, share, lanes = mid_ref.shape
    step = 2 * piece
    for block in range(width // lanes):
        rows = own_ref[:, :, :, block * lanes : (block + 1) * lanes]
        give_ref[:, block * step : (block + 1) * step] = rows.reshape(n_x, step, lanes)
    slot = (give_ref.shape[1] - step * (width // lanes)) // 3
    for which in range(3):
        at = step * (width // lanes) + which * slot
        for y in range(n_y):
            values = mid_ref[y, 1, which].astype(F32)
            values = jnp.concatenate([values, jnp.zeros((slot - share, lanes), F32)], axis=0)
            give_ref[y, at : at + slot] = values.astype(BF16)
    mixed, back = 0.0, 0.0
    for core, ref in enumerate((mine_ref, peer_ref)):
        hidden, gate_diff, up_diff = [all_units(mid_ref, core, which) for which in range(3)]
        mixed += dot(hidden, ref[2], 0, 0)
        back += dot(gate_diff, ref[0], 0, 0) + dot(up_diff, ref[1], 0, 0)
    out_ref[:, 0] = mixed.astype(out_ref.dtype).reshape(n_x, -1, width)
    out_ref[:, 1] = back.astype(out_ref.dtype).reshape(n_x, -1, width)


def weight_grads(mid_ref, got_ref, own_ref, down_hbm, gate_hbm, up_hbm, grad_ref, sems):
    n_x, _, piece, width = own_ref.shape
    n_y, _, _, share, lanes = mid_ref.shape
    step = 2 * piece
    base = step * (width // lanes)
    slot = (got_ref.shape[1] - base) // 3
    copies = []
    for which, hbm in enumerate((down_hbm, gate_hbm, up_hbm)):
        kind = 1 if which == 0 else 0
        far_rows = [
            got_ref[:, block * step + kind * piece : block * step + (kind + 1) * piece].reshape(n_x * piece, lanes)
            for block in range(width // lanes)
        ]
        rows = jnp.concatenate([own_ref[:, kind].reshape(-1, width), jnp.concatenate(far_rows, axis=1)], axis=0)
        at = base + which * slot
        far = [got_ref[y, at : at + slot].astype(F32)[:share] for y in range(n_y)]
        diff = jnp.concatenate([all_units(mid_ref, 0, which), jnp.concatenate(far, axis=0).astype(BF16)], axis=1)
        grad_ref[which] = dot(diff, rows, 1, 0).astype(BF16)
        copies.append(pltpu.make_async_copy(grad_ref.at[which], hbm, sems.at[which]))
        copies[-1].start()
    for copy in copies:
        copy.wait()


def call(body, inputs, *outs):
    return pl.pallas_call(
        body,
        out_shape=[jax.ShapeDtypeStruct(shape, dtype) for shape, dtype in outs],
        in_specs=[VMEM] * len(inputs),
        out_specs=[VMEM] * len(outs),
        compiler_params=LIMIT,
    )(*inputs)


def on_device(tokens, gate_weight, up_weight, down_weight, out_grad):
    rows, width = tokens.shape
    n_gx, n_x, n_y = lax.axis_size("gx"), lax.axis_size("x"), lax.axis_size("y")
    units = gate_weight.shape[1]
    mine = jnp.stack([gate_weight.T, up_weight.T, down_weight])
    peer = swap(mine, "core")

    both = jnp.concatenate([tokens, out_grad], axis=0)
    both = gather(both, "gx").reshape(n_gx, 2, rows, width).transpose(1, 0, 2, 3)
    own = gather(both.reshape(2, n_gx * rows, width), "x")

    first = scales(width)
    share = units // n_y
    half = n_x * n_gx * rows
    parts = call(functools.partial(partial_sums, first), (own, mine, peer), ((n_y, 2, 3, share, half), F32))[0]
    parts = lax.all_to_all(parts.astype(F16), "y", 0, 0).astype(F32).sum(axis=0) * (1.0 / n_y)
    away = parts.astype(F16)
    parts = parts + swap(away, "zh").astype(F32)
    gate_val, up_val, hidden_grad = [parts[:, i] * (n_y / first[i]) for i in range(3)]

    sig_val = jax.nn.sigmoid(gate_val)
    hidden = gate_val * sig_val * up_val
    up_diff = hidden_grad * gate_val * sig_val
    gate_diff = hidden_grad * up_val * sig_val * (1.0 + gate_val * (1.0 - sig_val))
    mid = jnp.stack([hidden.astype(BF16), gate_diff.astype(BF16), up_diff.astype(BF16)], axis=1)
    mid = gather(mid, "y")

    slot = -(-share // 16) * 16
    give = (n_x, own[0].size // half + 3 * slot, half)
    outs, give = call(partial_outs, (mid, own, mine, peer), (own.shape, BF16), (give, BF16))
    got = swap(give, "core")
    outs = lax.all_to_all(outs, "x", 0, 0).astype(F32).sum(axis=0)
    outs = outs.astype(BF16).reshape(2, n_gx, rows, width).transpose(1, 0, 2, 3)
    outs = outs.reshape(n_gx, 2 * rows, width)
    outs, got = lax.optimization_barrier((outs, got))
    outs = lax.all_to_all(outs, "gx", 0, 0).astype(F32).sum(axis=0).astype(BF16)

    grads = jax.ShapeDtypeStruct(down_weight.shape, BF16)
    down_grad, gate_grad, up_grad = pl.pallas_call(
        weight_grads,
        out_shape=[grads] * 3,
        in_specs=[VMEM] * 3,
        out_specs=[pl.BlockSpec(memory_space=pl.ANY)] * 3,
        scratch_shapes=[pltpu.VMEM((3,) + down_weight.shape, BF16), pltpu.SemaphoreType.DMA((3,))],
        compiler_params=LIMIT,
    )(mid, got, own)

    return (outs[:rows], outs[rows:], gate_grad.T, up_grad.T, down_grad)


def solution(mesh):
    fine = Mesh(mesh.devices.reshape(8, 4, 2, 2, 4), ("gx", "x", "core", "zh", "y"))
    hid, dim = ("gx", "x", "core"), ("zh", "y")
    act = P(hid, dim)
    return jax.shard_map(
        on_device,
        mesh=fine,
        in_specs=(act, P(dim, hid), P(dim, hid), act, act),
        out_specs=(act, act, P(dim, hid), P(dim, hid), act),
        check_vma=False,
    )
```

time: 125 us -> 122 us (0.976)
  blocking collectives: 88.5 us -> 74 us
  starting transfers between devices: 12 us -> 20.2 us
    all_to_all x1 -> x0, blocking collectives: 16.3 us -> none  [on_device(): outs = lax.all_to_all(outs, 'gx', 0, 0).astype(F32).sum(axis=0).astype(BF16)]
    all_to_all x0 -> x1, waiting for transfers between devices: none -> 9.81 us  [on_device(): outs = lax.all_to_all(outs, 'gx', 0, 0).astype(F32).sum(axis=0).astype(BF16)]
    ppermute x3, waiting for transfers between devices: 16.2 us -> 7.62 us  [swap(): return lax.ppermute(part, axis, [(0, 1), (1, 0)])]
    all_to_all x0 -> x1, starting transfers between devices: none -> 8.12 us  [on_device(): outs = lax.all_to_all(outs, 'gx', 0, 0).astype(F32).sum(axis=0).astype(BF16)]
    all_to_all x3, blocking collectives: 47.1 us -> 50.5 us  [gather(): lax.all_to_all(jnp.broadcast_to(part[None], (count,) + part.shape), axis,...]
    another operation x0 -> x1, other arithmetic: none -> 1.79 us  [on_device(): mine = jnp.stack([gate_weight.T, up_weight.T, down_weight])]
    all_to_all x1, blocking collectives: 12.4 us -> 10.6 us  [on_device(): lax.all_to_all(parts.astype(F16), 'y', 0, 0).astype(F32).sum(axis=0)]
  transfers between devices with their start and end apart: 3 -> 4, of which waited for: 3 -> 2; matrix products, arithmetic and copies ran while one was open for 0% -> 1% of each run, Pallas kernels for 2% -> 1%
where the time goes in v6:
time: 122 us; the launch traced here: 121 us
  blocking collectives  74 us (61%)
  starting transfers between devices  20.2 us (17%)
  waiting for transfers between devices  17.4 us (14%)
  Pallas kernels  4.1 us (3%)
  other arithmetic  2.21 us (2%)
  local copies, waits for them, and re-layouts  1.94 us (2%)
    all_to_all x3, blocking collectives, gather(): lax.all_to_all(jnp.broadcast_to(part[None], (count,) + part.shape), axis,...  50.5 us
    all_to_all x1, blocking collectives, on_device(): outs = lax.all_to_all(outs, 'x', 0, 0).astype(F32).sum(axis=0)  12.8 us
    ppermute x3, starting transfers between devices, swap(): return lax.ppermute(part, axis, [(0, 1), (1, 0)])  12.1 us
    all_to_all x1, blocking collectives, on_device(): lax.all_to_all(parts.astype(F16), 'y', 0, 0).astype(F32).sum(axis=0)  10.6 us
    all_to_all x1, waiting for transfers between devices, on_device(): outs = lax.all_to_all(outs, 'gx', 0, 0).astype(F32).sum(axis=0).astype(BF16)  9.81 us
    all_to_all x1, starting transfers between devices, on_device(): outs = lax.all_to_all(outs, 'gx', 0, 0).astype(F32).sum(axis=0).astype(BF16)  8.12 us
    ppermute x3, waiting for transfers between devices, swap(): return lax.ppermute(part, axis, [(0, 1), (1, 0)])  7.62 us
  transfers between devices with their start and end apart: 4, of which 2 were waited for; matrix products, arithmetic and copies ran while one was open for 1% of the time, Pallas kernels for 1%

profile of v6, /device:TPU:24, one launch (start us, length us, event | category | flops | bytes accessed | tf_op | source)
XLA Modules:
  0.0 120.6 jit_solution(731792395389022715)
XLA Ops:
  0.6 0.0 copy-start
  0.6 0.0 copy-start.1
  0.7 1.8 %pad_maximum_fusion.mine_ref = bf16[3,352,1024]{2,1,0:T(8,128)(2,1)S(1)} fusion(bf16[1,352,1024]{2,1,0:T(8,128)(2,1)} %bitcast.17, bf16[1,352,1024]{2,1,0:T(8,128)(2,1)} %bitcast.18, bf16[1,352,1024]{2,1,0:T(8,128)(2,1)} %bitcast.19), kind=kLoop, calls=%fused_computation | loop fusion | flops 2162688 | bytes 4325376 | tf_op jit(solution)/shard_map/stack | solution.py:115
  2.4 1.9 %collective-permute-start = (bf16[3,352,1024]{2,1,0:T(8,128)(2,1)S(1)}, bf16[3,352,1024]{2,1,0:T(8,128)(2,1)S(1)}, u32[]{:S(2)}, u32[]{:S(2)}) collective-permute-start(bf16[3,352,1024]{2,1,0:T(8,128)(2,1)S(1)} %pad_maximum_fusion.mine_ref), channel_id=1, source_target_pairs={{0,8},{8,0},{1,9},{9,1},{2,10},{10,2},{3,11},{11,3},{4,12},{12,4},... | collective-permute-start | bytes 6488072 | tf_op jit(solution)/shard_map/ppermute | solution.py:28
  4.4 0.0 copy-done
  4.4 24.9 %all_to_all.30 = bf16[8,8,1024]{2,1,0:T(8,128)(2,1)S(1)} all-to-all(bf16[8,8,1024]{2,1,0:T(8,128)(2,1)S(1)} %broadcast_in_dim.8), channel_id=1, replica_groups=mesh['gx'=8,'x'=4,'core'=2,'zh'=2,'y'=4] {'gx'}, dimensions={0} | all-to-all | bytes 262144 | tf_op jit(solution)/shard_map/all_to_all | solution.py:24
  29.3 0.1 copy.13
  29.4 0.1 copy.14
  29.6 0.1 broadcast_in_dim.10
  29.7 12.2 %all_to_all.31.rows_ref.own_ref = bf16[4,2,32,1024]{3,2,1,0:T(8,128)(2,1)S(1)} all-to-all(bf16[4,2,32,1024]{3,2,1,0:T(8,128)(2,1)S(1)} %broadcast_in_dim.10), channel_id=1, replica_groups=mesh['gx'=8,'x'=4,'core'=2,'zh'=2,'y'=4] {'x'}, dimensions={0} | all-to-all | bytes 1048576 | tf_op jit(solution)/shard_map/all_to_all | solution.py:24
  41.8 0.0 collective-permute-done.peer_ref
  41.8 1.3 %shard_map.92 = f32[4,2,3,88,128]{4,3,2,1,0:T(8,128)S(1)} custom-call(bf16[4,2,32,1024]{3,2,1,0:T(8,128)(2,1)S(1)} %all_to_all.31.rows_ref.own_ref, bf16[3,352,1024]{2,1,0:T(8,128)(2,1)S(1)} %pad_maximum_fusion.mine_ref, bf16[3,352,1024]{2,1,0:T(8,128)(2,1)S(1)} %collective-permute-done.peer_ref), custom_call_target="tpu_custom_call" | custom-call | tf_op jit(solution)/shard_map/pallas_call | solution.py:102
  43.1 0.1 convert_element_type.28
  43.2 10.6 %all_to_all.32 = f16[4,2,3,88,128]{4,3,2,1,0:T(8,128)(2,1)S(1)} all-to-all(f16[4,2,3,88,128]{4,3,2,1,0:T(8,128)(2,1)S(1)} %convert_element_type.28), channel_id=1, replica_groups=mesh['gx'=8,'x'=4,'core'=2,'zh'=2,'y'=4] {'y'}, dimensions={0} | all-to-all | bytes 1081344 | tf_op jit(solution)/shard_map/all_to_all | solution.py:126
  53.8 0.1 convert_reduce_fusion
  53.9 8.2 %collective-permute-start.1 = (f16[2,3,88,128]{3,2,1,0:T(8,128)(2,1)S(1)}, f16[2,3,88,128]{3,2,1,0:T(8,128)(2,1)S(1)}, u32[]{:S(2)}, u32[]{:S(2)}) collective-permute-start(f16[2,3,88,128]{3,2,1,0:T(8,128)(2,1)S(1)} %multiply_convert_fusion), channel_id=1, source_target_pairs={{0,4},{4,0},{1,5},{5,1},{2,6},{6,2},{3,7},{7,3},{8,12},{12,8},{9,1... | collective-permute-start | bytes 405512 | tf_op jit(solution)/shard_map/ppermute | solution.py:28
  62.1 7.6 %collective-permute-done.1 = f16[2,3,88,128]{3,2,1,0:T(8,128)(2,1)S(1)} collective-permute-done((f16[2,3,88,128]{3,2,1,0:T(8,128)(2,1)S(1)}, f16[2,3,88,128]{3,2,1,0:T(8,128)(2,1)S(1)}, u32[]{:S(2)}, u32[]{:S(2)}) %collective-permute-start.1) | collective-permute-done | bytes 135200 | tf_op jit(solution)/shard_map/ppermute | solution.py:28
  69.8 0.1 multiply_convert_fusion.3
  69.9 0.1 broadcast_in_dim.22
  70.0 13.5 %all_to_all.33.mid_ref = bf16[4,2,3,88,128]{4,3,2,1,0:T(8,128)(2,1)S(1)} all-to-all(bf16[4,2,3,88,128]{4,3,2,1,0:T(8,128)(2,1)S(1)} %broadcast_in_dim.22), channel_id=1, replica_groups=mesh['gx'=8,'x'=4,'core'=2,'zh'=2,'y'=4] {'y'}, dimensions={0} | all-to-all | bytes 1081344 | tf_op jit(solution)/shard_map/all_to_all | solution.py:24
  83.4 1.1 shard_map.93
  84.6 1.9 %collective-permute-start.2 = (bf16[4,800,128]{2,1,0:T(8,128)(2,1)S(1)}, bf16[4,800,128]{2,1,0:T(8,128)(2,1)S(1)}, u32[]{:S(2)}, u32[]{:S(2)}) collective-permute-start(bf16[4,800,128]{2,1,0:T(8,128)(2,1)S(1)} %get-tuple-element.13), channel_id=1, source_target_pairs={{0,8},{8,0},{1,9},{9,1},{2,10},{10,2},{3,11},{11,3},{4,12},{12,4},... | collective-permute-start | bytes 2457608 | tf_op jit(solution)/shard_map/ppermute | solution.py:28
  86.5 12.8 %all_to_all.34 = bf16[4,2,32,1024]{3,2,1,0:T(8,128)(2,1)S(1)} all-to-all(bf16[4,2,32,1024]{3,2,1,0:T(8,128)(2,1)S(1)} %get-tuple-element.12), channel_id=1, replica_groups=mesh['gx'=8,'x'=4,'core'=2,'zh'=2,'y'=4] {'x'}, dimensions={0} | all-to-all | bytes 1048576 | tf_op jit(solution)/shard_map/all_to_all | solution.py:142
  99.3 0.1 reduce_sum.34
  99.4 0.1 copy.16
  99.5 0.1 copy.17
  99.6 0.0 collective-permute-done.2.got_ref
  99.6 0.7 copy.18
  100.3 8.1 %all-to-all-start.5 = ((bf16[8,8,1024]{2,1,0:T(8,128)(2,1)}), bf16[8,8,1024]{2,1,0:T(8,128)(2,1)S(1)}, u32[]{:S(2)}, u32[]{:S(2)}) async-start(bf16[8,8,1024]{2,1,0:T(8,128)(2,1)} %copy.18), calls=%async_computation.5 | async-start | bytes 262144 | tf_op jit(solution)/shard_map/all_to_all | solution.py:146
  108.5 1.7 %shard_map.94 = (bf16[352,1024]{1,0:T(8,128)(2,1)}, bf16[352,1024]{1,0:T(8,128)(2,1)}, bf16[352,1024]{1,0:T(8,128)(2,1)}) custom-call(bf16[4,2,3,88,128]{4,3,2,1,0:T(8,128)(2,1)S(1)} %all_to_all.33.mid_ref, bf16[4,800,128]{2,1,0:T(8,128)(2,1)S(1)} %collective-permute-done.2.got_ref, bf16[4,2,32,1024]{3,2,1,0:T(8,128)(2,1)S(1)} %all_to_all.31.rows_ref.own_ref), custom_call_target="tpu_custom_call" | custom-call | tf_op jit(solution)/shard_map/pallas_call | solution.py:149
  110.2 9.8 %all-to-all-done.5 = bf16[8,8,1024]{2,1,0:T(8,128)(2,1)S(1)} async-done(((bf16[8,8,1024]{2,1,0:T(8,128)(2,1)}), bf16[8,8,1024]{2,1,0:T(8,128)(2,1)S(1)}, u32[]{:S(2)}, u32[]{:S(2)}) %all-to-all-start.5) | async-done | bytes 131104 | tf_op jit(solution)/shard_map/all_to_all | solution.py:146
  120.0 0.6 fusion
  (8 shorter events, 0.2 us)
Async XLA Ops:
  0.6 3.7 %copy-start = (bf16[4,1024]{1,0:T(4,128)(2,1)S(1)}, bf16[4,1024]{1,0:T(4,128)(2,1)}, u32[]{:S(2)}) copy-start(bf16[4,1024]{1,0:T(4,128)(2,1)} %param.9) | copy-start | bytes 24580
  0.6 3.7 %copy-start.1 = (bf16[4,1024]{1,0:T(4,128)(2,1)S(1)}, bf16[4,1024]{1,0:T(4,128)(2,1)}, u32[]{:S(2)}) copy-start(bf16[4,1024]{1,0:T(4,128)(2,1)} %param.5) | copy-start | bytes 24580
  2.4 39.4 %collective-permute-start = (bf16[3,352,1024]{2,1,0:T(8,128)(2,1)S(1)}, bf16[3,352,1024]{2,1,0:T(8,128)(2,1)S(1)}, u32[]{:S(2)}, u32[]{:S(2)}) collective-permute-start(bf16[3,352,1024]{2,1,0:T(8,128)(2,1)S(1)} %pad_maximum_fusion.mine_ref), channel_id=1, source_target_pairs={{0,8},{8,0},{1,9},{9,1},{2,10},{10,2},{3,11},{11,3},{4,12},{12,4},... | collective-permute-start | bytes 6488072 | tf_op jit(solution)/shard_map/ppermute | solution.py:28
  53.9 15.8 %collective-permute-start.1 = (f16[2,3,88,128]{3,2,1,0:T(8,128)(2,1)S(1)}, f16[2,3,88,128]{3,2,1,0:T(8,128)(2,1)S(1)}, u32[]{:S(2)}, u32[]{:S(2)}) collective-permute-start(f16[2,3,88,128]{3,2,1,0:T(8,128)(2,1)S(1)} %multiply_convert_fusion), channel_id=1, source_target_pairs={{0,4},{4,0},{1,5},{5,1},{2,6},{6,2},{3,7},{7,3},{8,12},{12,8},{9,1... | collective-permute-start | bytes 405512 | tf_op jit(solution)/shard_map/ppermute | solution.py:28
  84.6 15.1 %collective-permute-start.2 = (bf16[4,800,128]{2,1,0:T(8,128)(2,1)S(1)}, bf16[4,800,128]{2,1,0:T(8,128)(2,1)S(1)}, u32[]{:S(2)}, u32[]{:S(2)}) collective-permute-start(bf16[4,800,128]{2,1,0:T(8,128)(2,1)S(1)} %get-tuple-element.13), channel_id=1, source_target_pairs={{0,8},{8,0},{1,9},{9,1},{2,10},{10,2},{3,11},{11,3},{4,12},{12,4},... | collective-permute-start | bytes 2457608 | tf_op jit(solution)/shard_map/ppermute | solution.py:28
  100.3 19.6 %all-to-all-start.5 = ((bf16[8,8,1024]{2,1,0:T(8,128)(2,1)}), bf16[8,8,1024]{2,1,0:T(8,128)(2,1)S(1)}, u32[]{:S(2)}, u32[]{:S(2)}) async-start(bf16[8,8,1024]{2,1,0:T(8,128)(2,1)} %copy.18), calls=%async_computation.5 | async-start | bytes 262144 | tf_op jit(solution)/shard_map/all_to_all | solution.py:146

commit v7 on v6

--- a/solution.py
+++ b/solution.py
@@ -138,12 +138,12 @@
     slot = -(-share // 16) * 16
     give = (n_x, own[0].size // half + 3 * slot, half)
     outs, give = call(partial_outs, (mid, own, mine, peer), (own.shape, BF16), (give, BF16))
-    got = swap(give, "core")
     outs = lax.all_to_all(outs, "x", 0, 0).astype(F32).sum(axis=0)
     outs = outs.astype(BF16).reshape(2, n_gx, rows, width).transpose(1, 0, 2, 3)
     outs = outs.reshape(n_gx, 2 * rows, width)
-    outs, got = lax.optimization_barrier((outs, got))
-    outs = lax.all_to_all(outs, "gx", 0, 0).astype(F32).sum(axis=0).astype(BF16)
+    outs, give = lax.optimization_barrier((outs, give))
+    got = swap(give, "core")
+    outs = lax.all_to_all(outs, "gx", 0, 0)
 
     grads = jax.ShapeDtypeStruct(down_weight.shape, BF16)
     down_grad, gate_grad, up_grad = pl.pallas_call(
@@ -155,6 +155,8 @@
         compiler_params=LIMIT,
     )(mid, got, own)
 
+    outs, down_grad, gate_grad, up_grad = lax.optimization_barrier((outs, down_grad, gate_grad, up_grad))
+    outs = outs.astype(F32).sum(axis=0).astype(BF16)
     return (outs[:rows], outs[rows:], gate_grad.T, up_grad.T, down_grad)
 
 

time: 122 us -> 122 us (level)
  blocking collectives: 74 us -> 71.6 us
    all_to_all x1, blocking collectives: 12.8 us -> 10.5 us  [on_device(): outs = lax.all_to_all(outs, 'x', 0, 0).astype(F32).sum(axis=0)]
where the time goes in v7:
time: 122 us; the launch traced here: 120 us
  blocking collectives  71.6 us (59%)
  starting transfers between devices  21.2 us (17%)
  waiting for transfers between devices  18.5 us (15%)
  Pallas kernels  4.11 us (3%)
  other arithmetic  2.21 us (2%)
  local copies, waits for them, and re-layouts  1.94 us (2%)
    all_to_all x3, blocking collectives, gather(): lax.all_to_all(jnp.broadcast_to(part[None], (count,) + part.shape), axis,...  50.5 us
    ppermute x3, starting transfers between devices, swap(): return lax.ppermute(part, axis, [(0, 1), (1, 0)])  12.1 us
    all_to_all x1, waiting for transfers between devices, on_device(): outs = lax.all_to_all(outs, 'gx', 0, 0)  10.9 us
    all_to_all x1, blocking collectives, on_device(): lax.all_to_all(parts.astype(F16), 'y', 0, 0).astype(F32).sum(axis=0)  10.6 us
    all_to_all x1, blocking collectives, on_device(): outs = lax.all_to_all(outs, 'x', 0, 0).astype(F32).sum(axis=0)  10.5 us
    all_to_all x1, starting transfers between devices, on_device(): outs = lax.all_to_all(outs, 'gx', 0, 0)  9.13 us
    ppermute x3, waiting for transfers between devices, swap(): return lax.ppermute(part, axis, [(0, 1), (1, 0)])  7.62 us
  transfers between devices with their start and end apart: 4, of which 2 were waited for; matrix products, arithmetic and copies ran while one was open for 1% of the time, Pallas kernels for 1%

profile of v7, /device:TPU:24, one launch (start us, length us, event | category | flops | bytes accessed | tf_op | source)
XLA Modules:
  0.0 120.4 jit_solution(10338969482245467905)
XLA Ops:
  0.6 0.0 copy-start
  0.6 0.0 copy-start.1
  0.7 1.8 %pad_maximum_fusion.mine_ref = bf16[3,352,1024]{2,1,0:T(8,128)(2,1)S(1)} fusion(bf16[1,352,1024]{2,1,0:T(8,128)(2,1)} %bitcast.17, bf16[1,352,1024]{2,1,0:T(8,128)(2,1)} %bitcast.18, bf16[1,352,1024]{2,1,0:T(8,128)(2,1)} %bitcast.19), kind=kLoop, calls=%fused_computation | loop fusion | flops 2162688 | bytes 4325376 | tf_op jit(solution)/shard_map/stack | solution.py:115
  2.4 1.9 %collective-permute-start = (bf16[3,352,1024]{2,1,0:T(8,128)(2,1)S(1)}, bf16[3,352,1024]{2,1,0:T(8,128)(2,1)S(1)}, u32[]{:S(2)}, u32[]{:S(2)}) collective-permute-start(bf16[3,352,1024]{2,1,0:T(8,128)(2,1)S(1)} %pad_maximum_fusion.mine_ref), channel_id=1, source_target_pairs={{0,8},{8,0},{1,9},{9,1},{2,10},{10,2},{3,11},{11,3},{4,12},{12,4},... | collective-permute-start | bytes 6488072 | tf_op jit(solution)/shard_map/ppermute | solution.py:28
  4.4 0.0 copy-done
  4.4 24.9 %all_to_all.30 = bf16[8,8,1024]{2,1,0:T(8,128)(2,1)S(1)} all-to-all(bf16[8,8,1024]{2,1,0:T(8,128)(2,1)S(1)} %broadcast_in_dim.8), channel_id=1, replica_groups=mesh['gx'=8,'x'=4,'core'=2,'zh'=2,'y'=4] {'gx'}, dimensions={0} | all-to-all | bytes 262144 | tf_op jit(solution)/shard_map/all_to_all | solution.py:24
  29.3 0.1 copy.13
  29.4 0.1 copy.14
  29.6 0.1 broadcast_in_dim.10
  29.7 12.2 %all_to_all.31.rows_ref.own_ref = bf16[4,2,32,1024]{3,2,1,0:T(8,128)(2,1)S(1)} all-to-all(bf16[4,2,32,1024]{3,2,1,0:T(8,128)(2,1)S(1)} %broadcast_in_dim.10), channel_id=1, replica_groups=mesh['gx'=8,'x'=4,'core'=2,'zh'=2,'y'=4] {'x'}, dimensions={0} | all-to-all | bytes 1048576 | tf_op jit(solution)/shard_map/all_to_all | solution.py:24
  41.8 0.0 collective-permute-done.peer_ref
  41.8 1.3 %shard_map.92 = f32[4,2,3,88,128]{4,3,2,1,0:T(8,128)S(1)} custom-call(bf16[4,2,32,1024]{3,2,1,0:T(8,128)(2,1)S(1)} %all_to_all.31.rows_ref.own_ref, bf16[3,352,1024]{2,1,0:T(8,128)(2,1)S(1)} %pad_maximum_fusion.mine_ref, bf16[3,352,1024]{2,1,0:T(8,128)(2,1)S(1)} %collective-permute-done.peer_ref), custom_call_target="tpu_custom_call" | custom-call | tf_op jit(solution)/shard_map/pallas_call | solution.py:102
  43.1 0.1 convert_element_type.28
  43.2 10.6 %all_to_all.32 = f16[4,2,3,88,128]{4,3,2,1,0:T(8,128)(2,1)S(1)} all-to-all(f16[4,2,3,88,128]{4,3,2,1,0:T(8,128)(2,1)S(1)} %convert_element_type.28), channel_id=1, replica_groups=mesh['gx'=8,'x'=4,'core'=2,'zh'=2,'y'=4] {'y'}, dimensions={0} | all-to-all | bytes 1081344 | tf_op jit(solution)/shard_map/all_to_all | solution.py:126
  53.8 0.1 convert_reduce_fusion
  53.9 8.2 %collective-permute-start.1 = (f16[2,3,88,128]{3,2,1,0:T(8,128)(2,1)S(1)}, f16[2,3,88,128]{3,2,1,0:T(8,128)(2,1)S(1)}, u32[]{:S(2)}, u32[]{:S(2)}) collective-permute-start(f16[2,3,88,128]{3,2,1,0:T(8,128)(2,1)S(1)} %multiply_convert_fusion), channel_id=1, source_target_pairs={{0,4},{4,0},{1,5},{5,1},{2,6},{6,2},{3,7},{7,3},{8,12},{12,8},{9,1... | collective-permute-start | bytes 405512 | tf_op jit(solution)/shard_map/ppermute | solution.py:28
  62.1 7.6 %collective-permute-done.1 = f16[2,3,88,128]{3,2,1,0:T(8,128)(2,1)S(1)} collective-permute-done((f16[2,3,88,128]{3,2,1,0:T(8,128)(2,1)S(1)}, f16[2,3,88,128]{3,2,1,0:T(8,128)(2,1)S(1)}, u32[]{:S(2)}, u32[]{:S(2)}) %collective-permute-start.1) | collective-permute-done | bytes 135200 | tf_op jit(solution)/shard_map/ppermute | solution.py:28
  69.8 0.1 multiply_convert_fusion.3
  69.9 0.1 broadcast_in_dim.22
  70.0 13.5 %all_to_all.33.mid_ref = bf16[4,2,3,88,128]{4,3,2,1,0:T(8,128)(2,1)S(1)} all-to-all(bf16[4,2,3,88,128]{4,3,2,1,0:T(8,128)(2,1)S(1)} %broadcast_in_dim.22), channel_id=1, replica_groups=mesh['gx'=8,'x'=4,'core'=2,'zh'=2,'y'=4] {'y'}, dimensions={0} | all-to-all | bytes 1081344 | tf_op jit(solution)/shard_map/all_to_all | solution.py:24
  83.4 1.1 shard_map.93
  84.6 10.5 %all_to_all.34 = bf16[4,2,32,1024]{3,2,1,0:T(8,128)(2,1)S(1)} all-to-all(bf16[4,2,32,1024]{3,2,1,0:T(8,128)(2,1)S(1)} %get-tuple-element.16), channel_id=1, replica_groups=mesh['gx'=8,'x'=4,'core'=2,'zh'=2,'y'=4] {'x'}, dimensions={0} | all-to-all | bytes 1048576 | tf_op jit(solution)/shard_map/all_to_all | solution.py:141
  95.0 0.1 reduce_sum.34
  95.1 0.1 copy.16
  95.3 0.1 copy.17
  95.3 1.9 %collective-permute-start.2 = (bf16[4,800,128]{2,1,0:T(8,128)(2,1)S(1)}, bf16[4,800,128]{2,1,0:T(8,128)(2,1)S(1)}, u32[]{:S(2)}, u32[]{:S(2)}) collective-permute-start(bf16[4,800,128]{2,1,0:T(8,128)(2,1)S(1)} %get-tuple-element.19), channel_id=1, source_target_pairs={{0,8},{8,0},{1,9},{9,1},{2,10},{10,2},{3,11},{11,3},{4,12},{12,4},... | collective-permute-start | bytes 2457608 | tf_op jit(solution)/shard_map/ppermute | solution.py:28
  97.3 0.7 copy.18
  98.0 9.1 %all-to-all-start.5 = ((bf16[8,8,1024]{2,1,0:T(8,128)(2,1)}), bf16[8,8,1024]{2,1,0:T(8,128)(2,1)S(1)}, u32[]{:S(2)}, u32[]{:S(2)}) async-start(bf16[8,8,1024]{2,1,0:T(8,128)(2,1)} %copy.18), calls=%async_computation.5 | async-start | bytes 262144 | tf_op jit(solution)/shard_map/all_to_all | solution.py:146
  107.1 0.0 collective-permute-done.2.got_ref
  107.1 1.7 %shard_map.94 = (bf16[352,1024]{1,0:T(8,128)(2,1)}, bf16[352,1024]{1,0:T(8,128)(2,1)}, bf16[352,1024]{1,0:T(8,128)(2,1)}) custom-call(bf16[4,2,3,88,128]{4,3,2,1,0:T(8,128)(2,1)S(1)} %all_to_all.33.mid_ref, bf16[4,800,128]{2,1,0:T(8,128)(2,1)S(1)} %collective-permute-done.2.got_ref, bf16[4,2,32,1024]{3,2,1,0:T(8,128)(2,1)S(1)} %all_to_all.31.rows_ref.own_ref), custom_call_target="tpu_custom_call" | custom-call | tf_op jit(solution)/shard_map/pallas_call | solution.py:149
  108.9 10.9 %all-to-all-done.5 = bf16[8,8,1024]{2,1,0:T(8,128)(2,1)S(1)} async-done(((bf16[8,8,1024]{2,1,0:T(8,128)(2,1)}), bf16[8,8,1024]{2,1,0:T(8,128)(2,1)S(1)}, u32[]{:S(2)}, u32[]{:S(2)}) %all-to-all-start.5) | async-done | bytes 131104 | tf_op jit(solution)/shard_map/all_to_all | solution.py:146
  119.7 0.6 fusion
  (8 shorter events, 0.2 us)
Async XLA Ops:
  0.6 3.7 %copy-start = (bf16[4,1024]{1,0:T(4,128)(2,1)S(1)}, bf16[4,1024]{1,0:T(4,128)(2,1)}, u32[]{:S(2)}) copy-start(bf16[4,1024]{1,0:T(4,128)(2,1)} %param.9) | copy-start | bytes 24580
  0.6 3.7 %copy-start.1 = (bf16[4,1024]{1,0:T(4,128)(2,1)S(1)}, bf16[4,1024]{1,0:T(4,128)(2,1)}, u32[]{:S(2)}) copy-start(bf16[4,1024]{1,0:T(4,128)(2,1)} %param.5) | copy-start | bytes 24580
  2.4 39.4 %collective-permute-start = (bf16[3,352,1024]{2,1,0:T(8,128)(2,1)S(1)}, bf16[3,352,1024]{2,1,0:T(8,128)(2,1)S(1)}, u32[]{:S(2)}, u32[]{:S(2)}) collective-permute-start(bf16[3,352,1024]{2,1,0:T(8,128)(2,1)S(1)} %pad_maximum_fusion.mine_ref), channel_id=1, source_target_pairs={{0,8},{8,0},{1,9},{9,1},{2,10},{10,2},{3,11},{11,3},{4,12},{12,4},... | collective-permute-start | bytes 6488072 | tf_op jit(solution)/shard_map/ppermute | solution.py:28
  53.9 15.8 %collective-permute-start.1 = (f16[2,3,88,128]{3,2,1,0:T(8,128)(2,1)S(1)}, f16[2,3,88,128]{3,2,1,0:T(8,128)(2,1)S(1)}, u32[]{:S(2)}, u32[]{:S(2)}) collective-permute-start(f16[2,3,88,128]{3,2,1,0:T(8,128)(2,1)S(1)} %multiply_convert_fusion), channel_id=1, source_target_pairs={{0,4},{4,0},{1,5},{5,1},{2,6},{6,2},{3,7},{7,3},{8,12},{12,8},{9,1... | collective-permute-start | bytes 405512 | tf_op jit(solution)/shard_map/ppermute | solution.py:28
  95.3 11.8 %collective-permute-start.2 = (bf16[4,800,128]{2,1,0:T(8,128)(2,1)S(1)}, bf16[4,800,128]{2,1,0:T(8,128)(2,1)S(1)}, u32[]{:S(2)}, u32[]{:S(2)}) collective-permute-start(bf16[4,800,128]{2,1,0:T(8,128)(2,1)S(1)} %get-tuple-element.19), channel_id=1, source_target_pairs={{0,8},{8,0},{1,9},{9,1},{2,10},{10,2},{3,11},{11,3},{4,12},{12,4},... | collective-permute-start | bytes 2457608 | tf_op jit(solution)/shard_map/ppermute | solution.py:28
  98.0 21.7 %all-to-all-start.5 = ((bf16[8,8,1024]{2,1,0:T(8,128)(2,1)}), bf16[8,8,1024]{2,1,0:T(8,128)(2,1)S(1)}, u32[]{:S(2)}, u32[]{:S(2)}) async-start(bf16[8,8,1024]{2,1,0:T(8,128)(2,1)} %copy.18), calls=%async_computation.5 | async-start | bytes 262144 | tf_op jit(solution)/shard_map/all_to_all | solution.py:146

commit v8 on v7

--- a/solution.py
+++ b/solution.py
@@ -112,7 +112,9 @@
     rows, width = tokens.shape
     n_gx, n_x, n_y = lax.axis_size("gx"), lax.axis_size("x"), lax.axis_size("y")
     units = gate_weight.shape[1]
-    mine = jnp.stack([gate_weight.T, up_weight.T, down_weight])
+    mine = jnp.zeros((3,) + down_weight.shape, BF16)
+    for i, weight in enumerate((gate_weight.T, up_weight.T, down_weight)):
+        mine = lax.dynamic_update_index_in_dim(mine, weight, lax.optimization_barrier(jnp.int32(i)), 0)
     peer = swap(mine, "core")
 
     both = jnp.concatenate([tokens, out_grad], axis=0)

time: 122 us -> 122 us (level)
  other arithmetic: 2.21 us -> 0.42 us
  local copies, waits for them, and re-layouts: 1.94 us -> 3.48 us
    another operation x1 -> x0, other arithmetic: 1.79 us -> none  [on_device(): mine = jnp.stack([gate_weight.T, up_weight.T, down_weight])]
where the time goes in v8:
time: 122 us; the launch traced here: 120 us
  blocking collectives  71.6 us (59%)
  starting transfers between devices  21.2 us (17%)
  waiting for transfers between devices  18.5 us (15%)
  Pallas kernels  4.1 us (3%)
  local copies, waits for them, and re-layouts  3.48 us (3%)
    all_to_all x3, blocking collectives, gather(): lax.all_to_all(jnp.broadcast_to(part[None], (count,) + part.shape), axis,...  50.6 us
    ppermute x3, starting transfers between devices, swap(): return lax.ppermute(part, axis, [(0, 1), (1, 0)])  12.1 us
    all_to_all x1, waiting for transfers between devices, on_device(): outs = lax.all_to_all(outs, 'gx', 0, 0)  10.9 us
    all_to_all x1, blocking collectives, on_device(): lax.all_to_all(parts.astype(F16), 'y', 0, 0).astype(F32).sum(axis=0)  10.6 us
    all_to_all x1, blocking collectives, on_device(): outs = lax.all_to_all(outs, 'x', 0, 0).astype(F32).sum(axis=0)  10.5 us
    all_to_all x1, starting transfers between devices, on_device(): outs = lax.all_to_all(outs, 'gx', 0, 0)  9.13 us
    ppermute x3, waiting for transfers between devices, swap(): return lax.ppermute(part, axis, [(0, 1), (1, 0)])  7.62 us
  transfers between devices with their start and end apart: 4, of which 2 were waited for; matrix products, arithmetic and copies ran while one was open for 1% of the time, Pallas kernels for 1%

profile of v8, /device:TPU:24, one launch (start us, length us, event | category | flops | bytes accessed | tf_op | source)
XLA Modules:
  0.0 120.1 jit_solution(13129965262802601845)
XLA Ops:
  0.7 0.3 broadcast_in_dim.35
  0.9 0.8 copy-done
  1.7 0.1 bitcast_dynamic-update-slice_fusion.1
  1.8 0.1 copy-done.1
  2.0 0.1 bitcast_dynamic-update-slice_fusion
  2.0 0.2 copy-done.2
  2.2 0.1 bitcast_dynamic-update-slice_fusion.2.mine_ref
  2.2 1.9 %collective-permute-start = (bf16[3,352,1024]{2,1,0:T(8,128)(2,1)S(1)}, bf16[3,352,1024]{2,1,0:T(8,128)(2,1)S(1)}, u32[]{:S(2)}, u32[]{:S(2)}) collective-permute-start(bf16[3,352,1024]{2,1,0:T(8,128)(2,1)S(1)} %bitcast_dynamic-update-slice_fusion.2.mine_ref), channel_id=1, source_target_pairs={{0,8},{8,0},{1,9},{9,1},{2,10},{10,2},{3,11},{11,3},{4,12},{12,4},... | collective-permute-start | bytes 6488072 | tf_op jit(solution)/shard_map/ppermute | solution.py:28
  4.2 24.9 %all_to_all.30 = bf16[8,8,1024]{2,1,0:T(8,128)(2,1)S(1)} all-to-all(bf16[8,8,1024]{2,1,0:T(8,128)(2,1)S(1)} %broadcast_in_dim.32), channel_id=1, replica_groups=mesh['gx'=8,'x'=4,'core'=2,'zh'=2,'y'=4] {'gx'}, dimensions={0} | all-to-all | bytes 262144 | tf_op jit(solution)/shard_map/all_to_all | solution.py:24
  29.1 0.1 copy.13
  29.2 0.1 copy.14
  29.5 12.2 %all_to_all.31.rows_ref.own_ref = bf16[4,2,32,1024]{3,2,1,0:T(8,128)(2,1)S(1)} all-to-all(bf16[4,2,32,1024]{3,2,1,0:T(8,128)(2,1)S(1)} %broadcast_in_dim.34), channel_id=1, replica_groups=mesh['gx'=8,'x'=4,'core'=2,'zh'=2,'y'=4] {'x'}, dimensions={0} | all-to-all | bytes 1048576 | tf_op jit(solution)/shard_map/all_to_all | solution.py:24
  41.6 1.3 %shard_map.92 = f32[4,2,3,88,128]{4,3,2,1,0:T(8,128)S(1)} custom-call(bf16[4,2,32,1024]{3,2,1,0:T(8,128)(2,1)S(1)} %all_to_all.31.rows_ref.own_ref, bf16[3,352,1024]{2,1,0:T(8,128)(2,1)S(1)} %bitcast_dynamic-update-slice_fusion.2.mine_ref, bf16[3,352,1024]{2,1,0:T(8,128)(2,1)S(1)} %collective-permute-done.peer_ref), custom_call_target="tpu_custom_call" | custom-call | tf_op jit(solution)/shard_map/pallas_call | solution.py:102
  42.9 0.1 convert_element_type.28
  43.0 10.6 %all_to_all.32 = f16[4,2,3,88,128]{4,3,2,1,0:T(8,128)(2,1)S(1)} all-to-all(f16[4,2,3,88,128]{4,3,2,1,0:T(8,128)(2,1)S(1)} %convert_element_type.28), channel_id=1, replica_groups=mesh['gx'=8,'x'=4,'core'=2,'zh'=2,'y'=4] {'y'}, dimensions={0} | all-to-all | bytes 1081344 | tf_op jit(solution)/shard_map/all_to_all | solution.py:128
  53.6 0.1 convert_reduce_fusion
  53.7 8.2 %collective-permute-start.1 = (f16[2,3,88,128]{3,2,1,0:T(8,128)(2,1)S(1)}, f16[2,3,88,128]{3,2,1,0:T(8,128)(2,1)S(1)}, u32[]{:S(2)}, u32[]{:S(2)}) collective-permute-start(f16[2,3,88,128]{3,2,1,0:T(8,128)(2,1)S(1)} %multiply_convert_fusion), channel_id=1, source_target_pairs={{0,4},{4,0},{1,5},{5,1},{2,6},{6,2},{3,7},{7,3},{8,12},{12,8},{9,1... | collective-permute-start | bytes 405512 | tf_op jit(solution)/shard_map/ppermute | solution.py:28
  61.9 7.6 %collective-permute-done.1 = f16[2,3,88,128]{3,2,1,0:T(8,128)(2,1)S(1)} collective-permute-done((f16[2,3,88,128]{3,2,1,0:T(8,128)(2,1)S(1)}, f16[2,3,88,128]{3,2,1,0:T(8,128)(2,1)S(1)}, u32[]{:S(2)}, u32[]{:S(2)}) %collective-permute-start.1) | collective-permute-done | bytes 135200 | tf_op jit(solution)/shard_map/ppermute | solution.py:28
  69.6 0.1 multiply_convert_fusion.3
  69.7 0.1 broadcast_in_dim.39
  69.8 13.5 %all_to_all.33.mid_ref = bf16[4,2,3,88,128]{4,3,2,1,0:T(8,128)(2,1)S(1)} all-to-all(bf16[4,2,3,88,128]{4,3,2,1,0:T(8,128)(2,1)S(1)} %broadcast_in_dim.39), channel_id=1, replica_groups=mesh['gx'=8,'x'=4,'core'=2,'zh'=2,'y'=4] {'y'}, dimensions={0} | all-to-all | bytes 1081344 | tf_op jit(solution)/shard_map/all_to_all | solution.py:24
  83.2 1.1 shard_map.93
  84.4 10.5 %all_to_all.34 = bf16[4,2,32,1024]{3,2,1,0:T(8,128)(2,1)S(1)} all-to-all(bf16[4,2,32,1024]{3,2,1,0:T(8,128)(2,1)S(1)} %get-tuple-element.16), channel_id=1, replica_groups=mesh['gx'=8,'x'=4,'core'=2,'zh'=2,'y'=4] {'x'}, dimensions={0} | all-to-all | bytes 1048576 | tf_op jit(solution)/shard_map/all_to_all | solution.py:143
  94.8 0.1 reduce_sum.34
  94.9 0.1 copy.16
  95.1 0.1 copy.17
  95.1 1.9 %collective-permute-start.2 = (bf16[4,800,128]{2,1,0:T(8,128)(2,1)S(1)}, bf16[4,800,128]{2,1,0:T(8,128)(2,1)S(1)}, u32[]{:S(2)}, u32[]{:S(2)}) collective-permute-start(bf16[4,800,128]{2,1,0:T(8,128)(2,1)S(1)} %get-tuple-element.19), channel_id=1, source_target_pairs={{0,8},{8,0},{1,9},{9,1},{2,10},{10,2},{3,11},{11,3},{4,12},{12,4},... | collective-permute-start | bytes 2457608 | tf_op jit(solution)/shard_map/ppermute | solution.py:28
  97.1 0.7 copy.18
  97.8 9.1 %all-to-all-start.5 = ((bf16[8,8,1024]{2,1,0:T(8,128)(2,1)}), bf16[8,8,1024]{2,1,0:T(8,128)(2,1)S(1)}, u32[]{:S(2)}, u32[]{:S(2)}) async-start(bf16[8,8,1024]{2,1,0:T(8,128)(2,1)} %copy.18), calls=%async_computation.5 | async-start | bytes 262144 | tf_op jit(solution)/shard_map/all_to_all | solution.py:148
  106.9 1.7 %shard_map.94 = (bf16[352,1024]{1,0:T(8,128)(2,1)}, bf16[352,1024]{1,0:T(8,128)(2,1)}, bf16[352,1024]{1,0:T(8,128)(2,1)}) custom-call(bf16[4,2,3,88,128]{4,3,2,1,0:T(8,128)(2,1)S(1)} %all_to_all.33.mid_ref, bf16[4,800,128]{2,1,0:T(8,128)(2,1)S(1)} %collective-permute-done.2.got_ref, bf16[4,2,32,1024]{3,2,1,0:T(8,128)(2,1)S(1)} %all_to_all.31.rows_ref.own_ref), custom_call_target="tpu_custom_call" | custom-call | tf_op jit(solution)/shard_map/pallas_call | solution.py:151
  108.7 10.9 %all-to-all-done.5 = bf16[8,8,1024]{2,1,0:T(8,128)(2,1)S(1)} async-done(((bf16[8,8,1024]{2,1,0:T(8,128)(2,1)}), bf16[8,8,1024]{2,1,0:T(8,128)(2,1)S(1)}, u32[]{:S(2)}, u32[]{:S(2)}) %all-to-all-start.5) | async-done | bytes 131104 | tf_op jit(solution)/shard_map/all_to_all | solution.py:148
  119.5 0.6 fusion
  (17 shorter events, 0.2 us)
Async XLA Ops:
  0.6 1.1 copy-start
  0.6 1.3 %copy-start.1 = (bf16[1024,352]{0,1:T(8,128)(2,1)S(1)}, bf16[1024,352]{0,1:T(8,128)(2,1)}, u32[]{:S(2)}) copy-start(bf16[1024,352]{0,1:T(8,128)(2,1)} %param.7) | copy-start | bytes 2162692
  0.7 1.5 %copy-start.2 = (bf16[352,1024]{1,0:T(8,128)(2,1)S(1)}, bf16[352,1024]{1,0:T(8,128)(2,1)}, u32[]{:S(2)}) copy-start(bf16[352,1024]{1,0:T(8,128)(2,1)} %param.8) | copy-start | bytes 2162692
  1.7 2.4 %copy-start.3 = (bf16[4,1024]{1,0:T(4,128)(2,1)S(1)}, bf16[4,1024]{1,0:T(4,128)(2,1)}, u32[]{:S(2)}) copy-start(bf16[4,1024]{1,0:T(4,128)(2,1)} %param.9) | copy-start | bytes 24580
  1.7 2.4 %copy-start.4 = (bf16[4,1024]{1,0:T(4,128)(2,1)S(1)}, bf16[4,1024]{1,0:T(4,128)(2,1)}, u32[]{:S(2)}) copy-start(bf16[4,1024]{1,0:T(4,128)(2,1)} %param.5) | copy-start | bytes 24580
  2.2 39.4 %collective-permute-start = (bf16[3,352,1024]{2,1,0:T(8,128)(2,1)S(1)}, bf16[3,352,1024]{2,1,0:T(8,128)(2,1)S(1)}, u32[]{:S(2)}, u32[]{:S(2)}) collective-permute-start(bf16[3,352,1024]{2,1,0:T(8,128)(2,1)S(1)} %bitcast_dynamic-update-slice_fusion.2.mine_ref), channel_id=1, source_target_pairs={{0,8},{8,0},{1,9},{9,1},{2,10},{10,2},{3,11},{11,3},{4,12},{12,4},... | collective-permute-start | bytes 6488072 | tf_op jit(solution)/shard_map/ppermute | solution.py:28
  53.7 15.8 %collective-permute-start.1 = (f16[2,3,88,128]{3,2,1,0:T(8,128)(2,1)S(1)}, f16[2,3,88,128]{3,2,1,0:T(8,128)(2,1)S(1)}, u32[]{:S(2)}, u32[]{:S(2)}) collective-permute-start(f16[2,3,88,128]{3,2,1,0:T(8,128)(2,1)S(1)} %multiply_convert_fusion), channel_id=1, source_target_pairs={{0,4},{4,0},{1,5},{5,1},{2,6},{6,2},{3,7},{7,3},{8,12},{12,8},{9,1... | collective-permute-start | bytes 405512 | tf_op jit(solution)/shard_map/ppermute | solution.py:28
  95.1 11.8 %collective-permute-start.2 = (bf16[4,800,128]{2,1,0:T(8,128)(2,1)S(1)}, bf16[4,800,128]{2,1,0:T(8,128)(2,1)S(1)}, u32[]{:S(2)}, u32[]{:S(2)}) collective-permute-start(bf16[4,800,128]{2,1,0:T(8,128)(2,1)S(1)} %get-tuple-element.19), channel_id=1, source_target_pairs={{0,8},{8,0},{1,9},{9,1},{2,10},{10,2},{3,11},{11,3},{4,12},{12,4},... | collective-permute-start | bytes 2457608 | tf_op jit(solution)/shard_map/ppermute | solution.py:28
  97.8 21.7 %all-to-all-start.5 = ((bf16[8,8,1024]{2,1,0:T(8,128)(2,1)}), bf16[8,8,1024]{2,1,0:T(8,128)(2,1)S(1)}, u32[]{:S(2)}, u32[]{:S(2)}) async-start(bf16[8,8,1024]{2,1,0:T(8,128)(2,1)} %copy.18), calls=%async_computation.5 | async-start | bytes 262144 | tf_op jit(solution)/shard_map/all_to_all | solution.py:148

commit v9 on v8

--- a/solution.py
+++ b/solution.py
@@ -112,8 +112,8 @@
     rows, width = tokens.shape
     n_gx, n_x, n_y = lax.axis_size("gx"), lax.axis_size("x"), lax.axis_size("y")
     units = gate_weight.shape[1]
-    mine = jnp.zeros((3,) + down_weight.shape, BF16)
-    for i, weight in enumerate((gate_weight.T, up_weight.T, down_weight)):
+    mine = jnp.broadcast_to(down_weight[None], (3,) + down_weight.shape)
+    for i, weight in enumerate((gate_weight.T, up_weight.T)):
         mine = lax.dynamic_update_index_in_dim(mine, weight, lax.optimization_barrier(jnp.int32(i)), 0)
     peer = swap(mine, "core")
 

time: 122 us -> 122 us (level)
  no operation moved by 1% of the time
where the time goes in v9:
time: 122 us; the launch traced here: 121 us
  blocking collectives  71.6 us (59%)
  starting transfers between devices  21.2 us (17%)
  waiting for transfers between devices  18.5 us (15%)
  local copies, waits for them, and re-layouts  4.21 us (3%)
  Pallas kernels  4.1 us (3%)
    all_to_all x3, blocking collectives, gather(): lax.all_to_all(jnp.broadcast_to(part[None], (count,) + part.shape), axis,...  50.5 us
    ppermute x3, starting transfers between devices, swap(): return lax.ppermute(part, axis, [(0, 1), (1, 0)])  12.1 us
    all_to_all x1, waiting for transfers between devices, on_device(): outs = lax.all_to_all(outs, 'gx', 0, 0)  10.9 us
    all_to_all x1, blocking collectives, on_device(): lax.all_to_all(parts.astype(F16), 'y', 0, 0).astype(F32).sum(axis=0)  10.6 us
    all_to_all x1, blocking collectives, on_device(): outs = lax.all_to_all(outs, 'x', 0, 0).astype(F32).sum(axis=0)  10.5 us
    all_to_all x1, starting transfers between devices, on_device(): outs = lax.all_to_all(outs, 'gx', 0, 0)  9.13 us
    ppermute x3, waiting for transfers between devices, swap(): return lax.ppermute(part, axis, [(0, 1), (1, 0)])  7.62 us
  transfers between devices with their start and end apart: 4, of which 2 were waited for; matrix products, arithmetic and copies ran while one was open for 1% of the time, Pallas kernels for 1%

profile of v9, /device:TPU:24, one launch (start us, length us, event | category | flops | bytes accessed | tf_op | source)
XLA Modules:
  0.0 120.9 jit_solution(2791857927848393212)
XLA Ops:
  0.6 0.0 copy-start
  0.7 1.1 copy-done
  1.8 0.3 broadcast_in_dim.35
  2.1 0.1 bitcast_dynamic-update-slice_fusion.1
  2.1 0.8 copy-done.2
  2.9 0.1 bitcast_dynamic-update-slice_fusion.mine_ref
  3.0 1.9 %collective-permute-start = (bf16[3,352,1024]{2,1,0:T(8,128)(2,1)S(1)}, bf16[3,352,1024]{2,1,0:T(8,128)(2,1)S(1)}, u32[]{:S(2)}, u32[]{:S(2)}) collective-permute-start(bf16[3,352,1024]{2,1,0:T(8,128)(2,1)S(1)} %bitcast_dynamic-update-slice_fusion.mine_ref), channel_id=1, source_target_pairs={{0,8},{8,0},{1,9},{9,1},{2,10},{10,2},{3,11},{11,3},{4,12},{12,4},... | collective-permute-start | bytes 6488072 | tf_op jit(solution)/shard_map/ppermute | solution.py:28
  5.0 24.9 %all_to_all.30 = bf16[8,8,1024]{2,1,0:T(8,128)(2,1)S(1)} all-to-all(bf16[8,8,1024]{2,1,0:T(8,128)(2,1)S(1)} %broadcast_in_dim.32), channel_id=1, replica_groups=mesh['gx'=8,'x'=4,'core'=2,'zh'=2,'y'=4] {'gx'}, dimensions={0} | all-to-all | bytes 262144 | tf_op jit(solution)/shard_map/all_to_all | solution.py:24
  29.9 0.1 copy.13
  30.0 0.1 copy.14
  30.1 0.1 broadcast_in_dim.34
  30.2 12.2 %all_to_all.31.rows_ref.own_ref = bf16[4,2,32,1024]{3,2,1,0:T(8,128)(2,1)S(1)} all-to-all(bf16[4,2,32,1024]{3,2,1,0:T(8,128)(2,1)S(1)} %broadcast_in_dim.34), channel_id=1, replica_groups=mesh['gx'=8,'x'=4,'core'=2,'zh'=2,'y'=4] {'x'}, dimensions={0} | all-to-all | bytes 1048576 | tf_op jit(solution)/shard_map/all_to_all | solution.py:24
  42.4 1.3 %shard_map.92 = f32[4,2,3,88,128]{4,3,2,1,0:T(8,128)S(1)} custom-call(bf16[4,2,32,1024]{3,2,1,0:T(8,128)(2,1)S(1)} %all_to_all.31.rows_ref.own_ref, bf16[3,352,1024]{2,1,0:T(8,128)(2,1)S(1)} %bitcast_dynamic-update-slice_fusion.mine_ref, bf16[3,352,1024]{2,1,0:T(8,128)(2,1)S(1)} %collective-permute-done.peer_ref), custom_call_target="tpu_custom_call" | custom-call | tf_op jit(solution)/shard_map/pallas_call | solution.py:102
  43.6 0.1 convert_element_type.28
  43.7 10.6 %all_to_all.32 = f16[4,2,3,88,128]{4,3,2,1,0:T(8,128)(2,1)S(1)} all-to-all(f16[4,2,3,88,128]{4,3,2,1,0:T(8,128)(2,1)S(1)} %convert_element_type.28), channel_id=1, replica_groups=mesh['gx'=8,'x'=4,'core'=2,'zh'=2,'y'=4] {'y'}, dimensions={0} | all-to-all | bytes 1081344 | tf_op jit(solution)/shard_map/all_to_all | solution.py:128
  54.3 0.1 convert_reduce_fusion
  54.4 8.2 %collective-permute-start.1 = (f16[2,3,88,128]{3,2,1,0:T(8,128)(2,1)S(1)}, f16[2,3,88,128]{3,2,1,0:T(8,128)(2,1)S(1)}, u32[]{:S(2)}, u32[]{:S(2)}) collective-permute-start(f16[2,3,88,128]{3,2,1,0:T(8,128)(2,1)S(1)} %multiply_convert_fusion), channel_id=1, source_target_pairs={{0,4},{4,0},{1,5},{5,1},{2,6},{6,2},{3,7},{7,3},{8,12},{12,8},{9,1... | collective-permute-start | bytes 405512 | tf_op jit(solution)/shard_map/ppermute | solution.py:28
  62.7 7.6 %collective-permute-done.1 = f16[2,3,88,128]{3,2,1,0:T(8,128)(2,1)S(1)} collective-permute-done((f16[2,3,88,128]{3,2,1,0:T(8,128)(2,1)S(1)}, f16[2,3,88,128]{3,2,1,0:T(8,128)(2,1)S(1)}, u32[]{:S(2)}, u32[]{:S(2)}) %collective-permute-start.1) | collective-permute-done | bytes 135200 | tf_op jit(solution)/shard_map/ppermute | solution.py:28
  70.3 0.1 multiply_convert_fusion.3
  70.4 0.1 broadcast_in_dim.38
  70.5 13.5 %all_to_all.33.mid_ref = bf16[4,2,3,88,128]{4,3,2,1,0:T(8,128)(2,1)S(1)} all-to-all(bf16[4,2,3,88,128]{4,3,2,1,0:T(8,128)(2,1)S(1)} %broadcast_in_dim.38), channel_id=1, replica_groups=mesh['gx'=8,'x'=4,'core'=2,'zh'=2,'y'=4] {'y'}, dimensions={0} | all-to-all | bytes 1081344 | tf_op jit(solution)/shard_map/all_to_all | solution.py:24
  84.0 1.1 shard_map.93
  85.1 10.5 %all_to_all.34 = bf16[4,2,32,1024]{3,2,1,0:T(8,128)(2,1)S(1)} all-to-all(bf16[4,2,32,1024]{3,2,1,0:T(8,128)(2,1)S(1)} %get-tuple-element.16), channel_id=1, replica_groups=mesh['gx'=8,'x'=4,'core'=2,'zh'=2,'y'=4] {'x'}, dimensions={0} | all-to-all | bytes 1048576 | tf_op jit(solution)/shard_map/all_to_all | solution.py:143
  95.6 0.1 reduce_sum.34
  95.6 0.1 copy.16
  95.8 0.1 copy.17
  95.9 1.9 %collective-permute-start.2 = (bf16[4,800,128]{2,1,0:T(8,128)(2,1)S(1)}, bf16[4,800,128]{2,1,0:T(8,128)(2,1)S(1)}, u32[]{:S(2)}, u32[]{:S(2)}) collective-permute-start(bf16[4,800,128]{2,1,0:T(8,128)(2,1)S(1)} %get-tuple-element.19), channel_id=1, source_target_pairs={{0,8},{8,0},{1,9},{9,1},{2,10},{10,2},{3,11},{11,3},{4,12},{12,4},... | collective-permute-start | bytes 2457608 | tf_op jit(solution)/shard_map/ppermute | solution.py:28
  97.8 0.7 copy.18
  98.5 9.1 %all-to-all-start.5 = ((bf16[8,8,1024]{2,1,0:T(8,128)(2,1)}), bf16[8,8,1024]{2,1,0:T(8,128)(2,1)S(1)}, u32[]{:S(2)}, u32[]{:S(2)}) async-start(bf16[8,8,1024]{2,1,0:T(8,128)(2,1)} %copy.18), calls=%async_computation.5 | async-start | bytes 262144 | tf_op jit(solution)/shard_map/all_to_all | solution.py:148
  107.7 1.7 %shard_map.94 = (bf16[352,1024]{1,0:T(8,128)(2,1)}, bf16[352,1024]{1,0:T(8,128)(2,1)}, bf16[352,1024]{1,0:T(8,128)(2,1)}) custom-call(bf16[4,2,3,88,128]{4,3,2,1,0:T(8,128)(2,1)S(1)} %all_to_all.33.mid_ref, bf16[4,800,128]{2,1,0:T(8,128)(2,1)S(1)} %collective-permute-done.2.got_ref, bf16[4,2,32,1024]{3,2,1,0:T(8,128)(2,1)S(1)} %all_to_all.31.rows_ref.own_ref), custom_call_target="tpu_custom_call" | custom-call | tf_op jit(solution)/shard_map/pallas_call | solution.py:151
  109.4 10.9 %all-to-all-done.5 = bf16[8,8,1024]{2,1,0:T(8,128)(2,1)S(1)} async-done(((bf16[8,8,1024]{2,1,0:T(8,128)(2,1)}), bf16[8,8,1024]{2,1,0:T(8,128)(2,1)S(1)}, u32[]{:S(2)}, u32[]{:S(2)}) %all-to-all-start.5) | async-done | bytes 131104 | tf_op jit(solution)/shard_map/all_to_all | solution.py:148
  120.3 0.6 fusion
  (16 shorter events, 0.2 us)
Async XLA Ops:
  0.6 1.1 copy-start
  0.6 1.4 %copy-start.1 = (bf16[1024,352]{0,1:T(8,128)(2,1)S(1)}, bf16[1024,352]{0,1:T(8,128)(2,1)}, u32[]{:S(2)}) copy-start(bf16[1024,352]{0,1:T(8,128)(2,1)} %param.6) | copy-start | bytes 2162692
  1.7 1.2 copy-start.2
  2.0 2.9 %copy-start.3 = (bf16[4,1024]{1,0:T(4,128)(2,1)S(1)}, bf16[4,1024]{1,0:T(4,128)(2,1)}, u32[]{:S(2)}) copy-start(bf16[4,1024]{1,0:T(4,128)(2,1)} %param.9) | copy-start | bytes 24580
  2.0 2.9 %copy-start.4 = (bf16[4,1024]{1,0:T(4,128)(2,1)S(1)}, bf16[4,1024]{1,0:T(4,128)(2,1)}, u32[]{:S(2)}) copy-start(bf16[4,1024]{1,0:T(4,128)(2,1)} %param.5) | copy-start | bytes 24580
  3.0 39.4 %collective-permute-start = (bf16[3,352,1024]{2,1,0:T(8,128)(2,1)S(1)}, bf16[3,352,1024]{2,1,0:T(8,128)(2,1)S(1)}, u32[]{:S(2)}, u32[]{:S(2)}) collective-permute-start(bf16[3,352,1024]{2,1,0:T(8,128)(2,1)S(1)} %bitcast_dynamic-update-slice_fusion.mine_ref), channel_id=1, source_target_pairs={{0,8},{8,0},{1,9},{9,1},{2,10},{10,2},{3,11},{11,3},{4,12},{12,4},... | collective-permute-start | bytes 6488072 | tf_op jit(solution)/shard_map/ppermute | solution.py:28
  54.4 15.8 %collective-permute-start.1 = (f16[2,3,88,128]{3,2,1,0:T(8,128)(2,1)S(1)}, f16[2,3,88,128]{3,2,1,0:T(8,128)(2,1)S(1)}, u32[]{:S(2)}, u32[]{:S(2)}) collective-permute-start(f16[2,3,88,128]{3,2,1,0:T(8,128)(2,1)S(1)} %multiply_convert_fusion), channel_id=1, source_target_pairs={{0,4},{4,0},{1,5},{5,1},{2,6},{6,2},{3,7},{7,3},{8,12},{12,8},{9,1... | collective-permute-start | bytes 405512 | tf_op jit(solution)/shard_map/ppermute | solution.py:28
  95.9 11.8 %collective-permute-start.2 = (bf16[4,800,128]{2,1,0:T(8,128)(2,1)S(1)}, bf16[4,800,128]{2,1,0:T(8,128)(2,1)S(1)}, u32[]{:S(2)}, u32[]{:S(2)}) collective-permute-start(bf16[4,800,128]{2,1,0:T(8,128)(2,1)S(1)} %get-tuple-element.19), channel_id=1, source_target_pairs={{0,8},{8,0},{1,9},{9,1},{2,10},{10,2},{3,11},{11,3},{4,12},{12,4},... | collective-permute-start | bytes 2457608 | tf_op jit(solution)/shard_map/ppermute | solution.py:28
  98.5 21.7 %all-to-all-start.5 = ((bf16[8,8,1024]{2,1,0:T(8,128)(2,1)}), bf16[8,8,1024]{2,1,0:T(8,128)(2,1)S(1)}, u32[]{:S(2)}, u32[]{:S(2)}) async-start(bf16[8,8,1024]{2,1,0:T(8,128)(2,1)} %copy.18), calls=%async_computation.5 | async-start | bytes 262144 | tf_op jit(solution)/shard_map/all_to_all | solution.py:148
